TPU v7x, 32 devices: a whole 2x2x4 slice. The times are simulated.
32 devices in a mesh: dp: 4 (over z), seq: 8 (over y, x, core).
Axes of the slice: x: 2, y: 2, z: 4, core: 2. Of those that a mesh axis runs over, the one named last changes fastest.
Arguments:
- enc_input: bfloat16 [8, 512, 768], P('dp', 'seq'), may hold values from -6 to 6
- dec_input: bfloat16 [8, 512, 768], P('dp', 'seq'), may hold values from -6 to 6
- enc_lengths: int32 [8], P('dp'), may hold values from 128 to 512, as said below
- dec_lengths: int32 [8], P('dp'), may hold values from 128 to 512, as said below
- enc_buckets: int32 [1023], replicated, may hold values from 0 to 31
- dec_buckets: int32 [512], replicated, may hold values from 0 to 31
- attention_in: bfloat16 [3, 3, 768, 768], P(None, None, ('dp', 'seq')), may hold values from -0.21875 to 0.21875
- attention_out: bfloat16 [3, 768, 768], P(None, ('dp', 'seq')), may hold values from -0.875 to 0.875
- hidden_in: bfloat16 [2, 2, 768, 2048], P(None, None, ('dp', 'seq')), may hold values from -0.21875 to 0.21875
- hidden_out: bfloat16 [2, 2048, 768], P(None, ('dp', 'seq')), may hold values from -0.25 to 0.25
- norm_gains: bfloat16 [7, 768], P(None, ('dp', 'seq')), may hold values from 0.5 to 1.5
- position_bias: float32 [2, 32, 12], replicated, may hold values from -4 to 4
- enc_cotangent: bfloat16 [8, 512, 768], P('dp', 'seq'), may hold values from -6 to 6
- dec_cotangent: bfloat16 [8, 512, 768], P('dp', 'seq'), may hold values from -6 to 6
Outputs:
- enc_output: bfloat16 [8, 512, 768], P('dp', 'seq')
- dec_output: bfloat16 [8, 512, 768], P('dp', 'seq')
- grad_enc_input: float32 [8, 512, 768], P('dp', 'seq')
- grad_dec_input: float32 [8, 512, 768], P('dp', 'seq')
- grad_attention_in: float32 [3, 3, 768, 768], P(None, None, ('dp', 'seq'))
- grad_attention_out: float32 [3, 768, 768], P(None, ('dp', 'seq'))
- grad_hidden_in: float32 [2, 2, 768, 2048], P(None, None, ('dp', 'seq'))
- grad_hidden_out: float32 [2, 2048, 768], P(None, ('dp', 'seq'))
- grad_norm_gains: float32 [7, 768], P(None, ('dp', 'seq'))
- grad_position_bias: float32 [2, 32, 12], replicated
- row_attention_in: float32 [3, 3, 768], P(None, None, ('dp', 'seq'))
- col_attention_in: float32 [3, 3, 768], replicated
- row_attention_out: float32 [3, 768], P(None, ('dp', 'seq'))
- col_attention_out: float32 [3, 768], replicated
- row_hidden_in: float32 [2, 2, 768], P(None, None, ('dp', 'seq'))
- col_hidden_in: float32 [2, 2, 2048], replicated
- row_hidden_out: float32 [2, 2048], P(None, ('dp', 'seq'))
- col_hidden_out: float32 [2, 768], replicated
Inputs may be any that keep to these rules, and one draw needn't show every extreme that they name: `enc_lengths`: among the 2 sequences of one dp index at least one has all 512 valid tokens. `dec_lengths`: among the 2 sequences of one dp index at least one has all 512 valid tokens.
All inputs are finite; a program needn't handle non-finite values.
Results may differ from a plain program's by a relative error of at most 0.04.
Values may be sent and summed in bfloat16 or wider, within the bound.
No kernel may reach another device: no remote copies, remote signals or barrier semaphores. Data moves between devices by JAX's collectives and lax.ppermute only.
A program may use at most 384 MiB of HBM per device.

v0:
```python
import functools
import math

import jax
import jax.numpy as jnp
from jax import lax
from jax.experimental import pallas as pl
from jax.experimental.pallas import tpu as pltpu
from jax.sharding import Mesh, PartitionSpec as P

D = 768
HEADS = 12
HEAD = 64
FF = 2048


EPSILON = 1e-06
NEGATIVE = -1e30
HIGHEST = lax.Precision.HIGHEST


def rounded(values):
    return values.astype(jnp.bfloat16)


def rows_first(values):
    return values.transpose(0, 2, 1)


def rms_norm(values, gain_row):
    return (
        values * lax.rsqrt(jnp.mean(values * values, axis=-1, keepdims=True) + EPSILON) * gain_row
    )


def rms_back(values, gain_row, upstream):
    _, pullback = jax.vjp(rms_norm, values, gain_row)
    return pullback(upstream)


def gated_unit(gate_up):
    return jax.nn.gelu(gate_up[0], approximate=True) * gate_up[1]


def offset_table(buckets, layer_bias):
    choose = (buckets[:, None] == jnp.arange(layer_bias.shape[0], dtype=jnp.int32)[None, :]).astype(
        jnp.float32
    )
    return jnp.dot(choose, layer_bias, precision=HIGHEST).T


def bucket_grad(buckets, grad_bias, bucket_count):
    choose = (buckets[:, None] == jnp.arange(bucket_count, dtype=jnp.int32)[None, :]).astype(
        jnp.float32
    )
    return jnp.dot(choose.T, grad_bias.T, precision=HIGHEST)


def hankel_block(window, rows, cols):
    heads_here, length = (window.shape[0], window.shape[1])
    tiled = jnp.tile(window, (1, rows + 1))[:, : rows * (length + 1)]
    return tiled.reshape(heads_here, rows, length + 1)[:, :, :cols]


def bias_block(variant, table, row_start, col_start, rows, cols, extent):
    span = rows + cols - 1
    if variant == "enc":
        base = col_start - row_start - (rows - 1) + (extent - 1)
        window = lax.dynamic_slice_in_dim(table, base, span, 1)
        return hankel_block(window, rows, cols)[:, ::-1, :]
    widened = jnp.concatenate(
        [jnp.broadcast_to(table[:, :1], (table.shape[0], extent - 1)), table], axis=1
    )
    base = row_start - col_start - (cols - 1) + (extent - 1)
    window = lax.dynamic_slice_in_dim(widened, base, span, 1)
    return hankel_block(window, rows, cols)[:, :, ::-1]


def visible_mask(variant, row_ids, col_ids, lengths):
    visible = col_ids[None, None, :] < lengths[:, None, None]
    if variant == "dec":
        visible = visible & (col_ids[None, None, :] <= row_ids[None, :, None])
    return visible[:, None]


def block_scores(query_heads, key_heads, row_ids, col_ids, lengths, variant, offset_bias, extent):
    factor = HEAD ** (-0.5)
    scores = (
        jnp.einsum("sqhe,skhe->shqk", query_heads, key_heads, preferred_element_type=jnp.float32)
        * factor
    )
    if offset_bias is not None:
        scores = (
            scores
            + bias_block(
                variant,
                offset_bias,
                row_ids[0],
                col_ids[0],
                row_ids.shape[0],
                col_ids.shape[0],
                extent,
            )[None]
        )
    return (scores, visible_mask(variant, row_ids, col_ids, lengths))


def row_products(grad_context, context):
    seqs_here, rows_here = (context.shape[0], context.shape[1])
    return jnp.sum(
        (grad_context.astype(jnp.float32) * context).reshape(seqs_here, rows_here, HEADS, HEAD),
        axis=-1,
    ).transpose(0, 2, 1)


def attend(queries, row_ids, lengths, variant, offset_bias, extent, fold_keys):
    seqs_here, rows_here = (queries.shape[0], queries.shape[1])
    query_heads = queries.reshape(seqs_here, rows_here, HEADS, HEAD)

    def fold_step(carried, pieces, begin_at):
        key_rows, value_rows = pieces
        block_len = math.gcd(key_rows.shape[1], 512)

        def block_step(block_id, running):
            row_max, row_sum, weighted = running
            offset_in = block_id * block_len
            key_heads = lax.dynamic_slice_in_dim(key_rows, offset_in, block_len, 1).reshape(
                seqs_here, block_len, HEADS, HEAD
            )
            value_heads = lax.dynamic_slice_in_dim(value_rows, offset_in, block_len, 1).reshape(
                seqs_here, block_len, HEADS, HEAD
            )
            col_ids = offset_in + jnp.arange(block_len, dtype=jnp.int32)
            scores, visible = block_scores(
                query_heads, key_heads, row_ids, col_ids, lengths, variant, offset_bias, extent
            )
            new_max = jnp.maximum(row_max, jnp.max(jnp.where(visible, scores, NEGATIVE), axis=-1))
            weights = jnp.where(visible, jnp.exp(scores - new_max[..., None]), 0.0)
            shrink = jnp.exp(row_max - new_max)
            row_sum = row_sum * shrink + jnp.sum(weights, axis=-1)
            weighted = weighted * shrink[..., None] + jnp.einsum(
                "shqk,skhe->shqe", rounded(weights), value_heads, preferred_element_type=jnp.float32
            )
            return (new_max, row_sum, weighted)

        return lax.fori_loop(0, key_rows.shape[1] // block_len, block_step, carried)

    initial = (
        jnp.full((seqs_here, HEADS, rows_here), NEGATIVE, jnp.float32),
        jnp.zeros((seqs_here, HEADS, rows_here), jnp.float32),
        jnp.zeros((seqs_here, HEADS, rows_here, HEAD), jnp.float32),
    )
    row_max, row_sum, weighted = fold_keys(fold_step, initial)
    context = (
        (weighted / row_sum[..., None])
        .transpose(0, 2, 1, 3)
        .reshape(seqs_here, rows_here, HEADS * HEAD)
    )
    return (context, row_max + jnp.log(row_sum))


def attend_back(
    queries,
    log_sums,
    row_dots,
    grad_context,
    row_ids,
    lengths,
    variant,
    offset_bias,
    extent,
    fold_keys,
):
    seqs_here, rows_here = (queries.shape[0], queries.shape[1])
    query_heads = queries.reshape(seqs_here, rows_here, HEADS, HEAD)
    grad_heads = grad_context.reshape(seqs_here, rows_here, HEADS, HEAD)
    bias_width = offset_bias.shape[1] if offset_bias is not None else 1
    factor = HEAD ** (-0.5)

    def fold_step(carried, pieces, begin_at):
        key_rows, value_rows = pieces
        block_len = math.gcd(key_rows.shape[1], 512)

        def block_step(block_id, running):
            grad_query, grad_bias = (running[0], running[-1])
            offset_in = block_id * block_len
            key_heads = lax.dynamic_slice_in_dim(key_rows, offset_in, block_len, 1).reshape(
                seqs_here, block_len, HEADS, HEAD
            )
            value_heads = lax.dynamic_slice_in_dim(value_rows, offset_in, block_len, 1).reshape(
                seqs_here, block_len, HEADS, HEAD
            )
            col_ids = offset_in + jnp.arange(block_len, dtype=jnp.int32)
            scores, visible = block_scores(
                query_heads, key_heads, row_ids, col_ids, lengths, variant, offset_bias, extent
            )
            weights = jnp.where(visible, jnp.exp(scores - log_sums[..., None]), 0.0)
            grad_weights = jnp.einsum(
                "sqhe,skhe->shqk", grad_heads, value_heads, preferred_element_type=jnp.float32
            )
            grad_scores = weights * (grad_weights - row_dots[..., None])
            if offset_bias is not None:

                def table_block(table_values):
                    return bias_block(
                        variant,
                        table_values,
                        row_ids[0],
                        col_ids[0],
                        row_ids.shape[0],
                        col_ids.shape[0],
                        extent,
                    )

                _, table_pull = jax.vjp(table_block, offset_bias)
                grad_bias = grad_bias + table_pull(jnp.sum(grad_scores, axis=0))[0]
            grad_raw = rounded(grad_scores * factor)
            grad_query = grad_query + jnp.einsum(
                "shqk,skhe->shqe", grad_raw, key_heads, preferred_element_type=jnp.float32
            )
            return (grad_query, grad_bias)

        return lax.fori_loop(0, key_rows.shape[1] // block_len, block_step, carried)

    query_start = jnp.zeros((seqs_here, HEADS, rows_here, HEAD), jnp.float32)
    bias_start = jnp.zeros((HEADS, bias_width), jnp.float32)
    initial = (query_start, bias_start)
    result = fold_keys(fold_step, initial)
    grad_query = result[0].transpose(0, 2, 1, 3).reshape(seqs_here, rows_here, HEADS * HEAD)
    return (grad_query, None, None, result[1])


def owned_key_grads(
    key_rows, value_rows, col_ids, lengths, variant, offset_bias, extent, fold_queries
):
    seqs_here, keys_here = (key_rows.shape[0], key_rows.shape[1])
    key_heads = key_rows.reshape(seqs_here, keys_here, HEADS, HEAD)
    value_heads = value_rows.reshape(seqs_here, keys_here, HEADS, HEAD)
    factor = HEAD ** (-0.5)

    def fold_step(carried, pieces, begin_at):
        query_rows, grad_rows, log_rows, dot_rows = pieces
        block_len = math.gcd(query_rows.shape[1], 512)

        def block_step(block_id, running):
            grad_keys, grad_values = running
            offset_in = block_id * block_len
            query_heads = lax.dynamic_slice_in_dim(query_rows, offset_in, block_len, 1).reshape(
                seqs_here, block_len, HEADS, HEAD
            )
            grad_heads = lax.dynamic_slice_in_dim(grad_rows, offset_in, block_len, 1).reshape(
                seqs_here, block_len, HEADS, HEAD
            )
            log_block = lax.dynamic_slice_in_dim(log_rows, offset_in, block_len, 1).transpose(
                0, 2, 1
            )
            dot_block = lax.dynamic_slice_in_dim(dot_rows, offset_in, block_len, 1).transpose(
                0, 2, 1
            )
            row_ids = offset_in + jnp.arange(block_len, dtype=jnp.int32)
            scores, visible = block_scores(
                query_heads, key_heads, row_ids, col_ids, lengths, variant, offset_bias, extent
            )
            weights = jnp.where(visible, jnp.exp(scores - log_block[..., None]), 0.0)
            grad_weights = jnp.einsum(
                "sqhe,skhe->shqk", grad_heads, value_heads, preferred_element_type=jnp.float32
            )
            grad_scores = weights * (grad_weights - dot_block[..., None])
            grad_raw = rounded(grad_scores * factor)
            grad_keys = grad_keys + jnp.einsum(
                "shqk,sqhe->skhe", grad_raw, query_heads, preferred_element_type=jnp.float32
            ).reshape(seqs_here, keys_here, HEADS * HEAD)
            grad_values = grad_values + jnp.einsum(
                "shqk,sqhe->skhe", rounded(weights), grad_heads, preferred_element_type=jnp.float32
            ).reshape(seqs_here, keys_here, HEADS * HEAD)
            return (grad_keys, grad_values)

        return lax.fori_loop(0, query_rows.shape[1] // block_len, block_step, carried)

    initial = (
        jnp.zeros((seqs_here, keys_here, HEADS * HEAD), jnp.float32),
        jnp.zeros((seqs_here, keys_here, HEADS * HEAD), jnp.float32),
    )
    return fold_queries(fold_step, initial)


def feed_forward(residual, gain_row, weights_in, weights_out):
    normed_low = rounded(rms_norm(residual, gain_row))
    gate_up = jnp.einsum(
        "srd,jdf->jsrf", normed_low, weights_in, preferred_element_type=jnp.float32
    )
    hidden = rounded(gated_unit(gate_up))
    output = jnp.einsum("srf,fd->srd", hidden, weights_out, preferred_element_type=jnp.float32)
    return (residual + output, (normed_low, gate_up, hidden))


def feed_back(residual, gain_row, weights_in, weights_out, kept_values, upstream):
    normed_low, gate_up, hidden = kept_values
    upstream_low = rounded(upstream)
    grad_out_weights = jnp.einsum(
        "srf,srd->fd", hidden, upstream_low, preferred_element_type=jnp.float32
    )
    grad_hidden = jnp.einsum(
        "srd,fd->srf", upstream_low, weights_out, preferred_element_type=jnp.float32
    )
    _, pullback = jax.vjp(gated_unit, gate_up)
    grad_gate_up = rounded(pullback(grad_hidden)[0])
    grad_in_weights = jnp.einsum(
        "srd,jsrf->jdf", normed_low, grad_gate_up, preferred_element_type=jnp.float32
    )
    grad_normed = jnp.einsum(
        "jsrf,jdf->srd", grad_gate_up, weights_in, preferred_element_type=jnp.float32
    )
    grad_residual, grad_gain = rms_back(residual, gain_row, grad_normed)
    return (upstream + grad_residual, grad_gain, grad_in_weights, grad_out_weights)


def local(
    enc_input,
    dec_input,
    enc_lengths,
    dec_lengths,
    enc_buckets,
    dec_buckets,
    attention_in,
    attention_out,
    hidden_in,
    hidden_out,
    norm_gains,
    position_bias,
    enc_cotangent,
    dec_cotangent,
):
    full_in, full_out, full_hidden_in, full_hidden_out, full_gains = (
        lax.all_gather(attention_in, ("dp", "seq"), axis=2, tiled=True),
        lax.all_gather(attention_out, ("dp", "seq"), axis=1, tiled=True),
        lax.all_gather(hidden_in, ("dp", "seq"), axis=2, tiled=True),
        lax.all_gather(hidden_out, ("dp", "seq"), axis=1, tiled=True),
        lax.all_gather(norm_gains, ("dp", "seq"), axis=1, tiled=True),
    )
    gain_rows = full_gains.astype(jnp.float32)
    enc_rows = enc_input.shape[1]
    dec_rows = dec_input.shape[1]
    seq_index = lax.axis_index("seq")
    enc_ids = seq_index * enc_rows + jnp.arange(enc_rows, dtype=jnp.int32)
    dec_ids = seq_index * dec_rows + jnp.arange(dec_rows, dtype=jnp.int32)
    enc_extent = (enc_buckets.shape[0] + 1) // 2
    dec_extent = dec_buckets.shape[0]
    enc_table = offset_table(enc_buckets, position_bias[0])
    dec_table = offset_table(dec_buckets, position_bias[1])
    enc_values = enc_input.astype(jnp.float32)
    norm_a_low = rounded(rms_norm(enc_values, gain_rows[0]))
    enc_qkv = rounded(
        jnp.einsum("srd,jde->jsre", norm_a_low, full_in[0], preferred_element_type=jnp.float32)
    )
    enc_context, enc_logs = attend(
        enc_qkv[0],
        enc_ids,
        enc_lengths,
        "enc",
        enc_table,
        enc_extent,
        lambda folder, initial: folder(
            initial,
            (
                lax.all_gather(enc_qkv[1], "seq", axis=1, tiled=True),
                lax.all_gather(enc_qkv[2], "seq", axis=1, tiled=True),
            ),
            jnp.int32(0),
        ),
    )
    enc_context_low = rounded(enc_context)
    enc_mid = enc_values + jnp.einsum(
        "srd,de->sre", enc_context_low, full_out[0], preferred_element_type=jnp.float32
    )
    enc_last, enc_ffn_kept = feed_forward(
        enc_mid, gain_rows[1], full_hidden_in[0], full_hidden_out[0]
    )
    memory = rms_norm(enc_last, gain_rows[2])
    memory_low = rounded(memory)
    dec_values = dec_input.astype(jnp.float32)
    norm_b_low = rounded(rms_norm(dec_values, gain_rows[3]))
    dec_qkv = rounded(
        jnp.einsum("srd,jde->jsre", norm_b_low, full_in[1], preferred_element_type=jnp.float32)
    )
    dec_context, dec_logs = attend(
        dec_qkv[0],
        dec_ids,
        dec_lengths,
        "dec",
        dec_table,
        dec_extent,
        lambda folder, initial: folder(
            initial,
            (
                lax.all_gather(dec_qkv[1], "seq", axis=1, tiled=True),
                lax.all_gather(dec_qkv[2], "seq", axis=1, tiled=True),
            ),
            jnp.int32(0),
        ),
    )
    dec_context_low = rounded(dec_context)
    dec_mid = dec_values + jnp.einsum(
        "srd,de->sre", dec_context_low, full_out[1], preferred_element_type=jnp.float32
    )
    norm_c_low = rounded(rms_norm(dec_mid, gain_rows[4]))
    cross_query = rounded(
        jnp.einsum("srd,de->sre", norm_c_low, full_in[2, 0], preferred_element_type=jnp.float32)
    )
    cross_pair = rounded(
        jnp.einsum("srd,jde->jsre", memory_low, full_in[2, 1:], preferred_element_type=jnp.float32)
    )
    cross_context, cross_logs = attend(
        cross_query,
        dec_ids,
        enc_lengths,
        "cross",
        None,
        0,
        lambda folder, initial: folder(
            initial,
            (
                lax.all_gather(cross_pair[0], "seq", axis=1, tiled=True),
                lax.all_gather(cross_pair[1], "seq", axis=1, tiled=True),
            ),
            jnp.int32(0),
        ),
    )
    cross_low = rounded(cross_context)
    dec_cross = dec_mid + jnp.einsum(
        "srd,de->sre", cross_low, full_out[2], preferred_element_type=jnp.float32
    )
    dec_last, dec_ffn_kept = feed_forward(
        dec_cross, gain_rows[5], full_hidden_in[1], full_hidden_out[1]
    )
    dec_final = rms_norm(dec_last, gain_rows[6])
    grad_dec_last, grad_gain_six = rms_back(
        dec_last, gain_rows[6], dec_cotangent.astype(jnp.float32)
    )
    grad_dec_cross, grad_gain_five, grad_hin_one, grad_hout_one = feed_back(
        dec_cross, gain_rows[5], full_hidden_in[1], full_hidden_out[1], dec_ffn_kept, grad_dec_last
    )
    upstream_low = rounded(grad_dec_cross)
    grad_out_two = jnp.einsum(
        "srd,sre->de", cross_low, upstream_low, preferred_element_type=jnp.float32
    )
    grad_cross_context = rounded(
        jnp.einsum("sre,de->srd", upstream_low, full_out[2], preferred_element_type=jnp.float32)
    )
    cross_dots = row_products(grad_cross_context, cross_context)
    cross_grad_query, cross_grad_keys, cross_grad_values, _ = attend_back(
        cross_query,
        cross_logs,
        cross_dots,
        grad_cross_context,
        dec_ids,
        enc_lengths,
        "cross",
        None,
        0,
        lambda folder, initial: folder(
            initial,
            (
                lax.all_gather(cross_pair[0], "seq", axis=1, tiled=True),
                lax.all_gather(cross_pair[1], "seq", axis=1, tiled=True),
            ),
            jnp.int32(0),
        ),
    )
    cross_query_low = rounded(cross_grad_query)
    grad_query_two = jnp.einsum(
        "srd,sre->de", norm_c_low, cross_query_low, preferred_element_type=jnp.float32
    )
    grad_norm_c = jnp.einsum(
        "sre,de->srd", cross_query_low, full_in[2, 0], preferred_element_type=jnp.float32
    )
    grad_mid_part, grad_gain_four = rms_back(dec_mid, gain_rows[4], grad_norm_c)
    grad_dec_mid = grad_dec_cross + grad_mid_part
    upstream_low = rounded(grad_dec_mid)
    grad_out_one = jnp.einsum(
        "srd,sre->de", dec_context_low, upstream_low, preferred_element_type=jnp.float32
    )
    grad_dec_context = rounded(
        jnp.einsum("sre,de->srd", upstream_low, full_out[1], preferred_element_type=jnp.float32)
    )
    dec_dots = row_products(grad_dec_context, dec_context)
    dec_grad_query, dec_grad_keys, dec_grad_values, grad_dec_bias = attend_back(
        dec_qkv[0],
        dec_logs,
        dec_dots,
        grad_dec_context,
        dec_ids,
        dec_lengths,
        "dec",
        dec_table,
        dec_extent,
        lambda folder, initial: folder(
            initial,
            (
                lax.all_gather(dec_qkv[1], "seq", axis=1, tiled=True),
                lax.all_gather(dec_qkv[2], "seq", axis=1, tiled=True),
            ),
            jnp.int32(0),
        ),
    )
    cross_key_grad, cross_value_grad = owned_key_grads(
        cross_pair[0],
        cross_pair[1],
        enc_ids,
        enc_lengths,
        "cross",
        None,
        0,
        lambda folder, initial: folder(
            initial,
            (
                lax.all_gather(cross_query, "seq", axis=1, tiled=True),
                lax.all_gather(grad_cross_context, "seq", axis=1, tiled=True),
                lax.all_gather(
                    rows_first(cross_logs).astype(jnp.bfloat16), "seq", axis=1, tiled=True
                ).astype(jnp.float32),
                lax.all_gather(
                    rows_first(cross_dots).astype(jnp.bfloat16), "seq", axis=1, tiled=True
                ).astype(jnp.float32),
            ),
            jnp.int32(0),
        ),
    )
    dec_key_grad, dec_value_grad = owned_key_grads(
        dec_qkv[1],
        dec_qkv[2],
        dec_ids,
        dec_lengths,
        "dec",
        dec_table,
        dec_extent,
        lambda folder, initial: folder(
            initial,
            (
                lax.all_gather(dec_qkv[0], "seq", axis=1, tiled=True),
                lax.all_gather(grad_dec_context, "seq", axis=1, tiled=True),
                lax.all_gather(
                    rows_first(dec_logs).astype(jnp.bfloat16), "seq", axis=1, tiled=True
                ).astype(jnp.float32),
                lax.all_gather(
                    rows_first(dec_dots).astype(jnp.bfloat16), "seq", axis=1, tiled=True
                ).astype(jnp.float32),
            ),
            jnp.int32(0),
        ),
    )
    pair_grads = rounded(jnp.stack([cross_key_grad, cross_value_grad]))
    grad_pair_two = jnp.einsum(
        "srd,jsre->jde", memory_low, pair_grads, preferred_element_type=jnp.float32
    )
    grad_memory = jnp.einsum(
        "jsre,jde->srd", pair_grads, full_in[2, 1:], preferred_element_type=jnp.float32
    )
    dec_grads = rounded(jnp.stack([dec_grad_query, dec_key_grad, dec_value_grad]))
    grad_in_one = jnp.einsum(
        "srd,jsre->jde", norm_b_low, dec_grads, preferred_element_type=jnp.float32
    )
    grad_norm_b = jnp.einsum(
        "jsre,jde->srd", dec_grads, full_in[1], preferred_element_type=jnp.float32
    )
    grad_dec_part, grad_gain_three = rms_back(dec_values, gain_rows[3], grad_norm_b)
    grad_dec_input = grad_dec_mid + grad_dec_part
    grad_memory_total = enc_cotangent.astype(jnp.float32) + grad_memory
    grad_enc_last, grad_gain_two = rms_back(enc_last, gain_rows[2], grad_memory_total)
    grad_enc_mid, grad_gain_one, grad_hin_zero, grad_hout_zero = feed_back(
        enc_mid, gain_rows[1], full_hidden_in[0], full_hidden_out[0], enc_ffn_kept, grad_enc_last
    )
    upstream_low = rounded(grad_enc_mid)
    grad_out_zero = jnp.einsum(
        "srd,sre->de", enc_context_low, upstream_low, preferred_element_type=jnp.float32
    )
    grad_enc_context = rounded(
        jnp.einsum("sre,de->srd", upstream_low, full_out[0], preferred_element_type=jnp.float32)
    )
    enc_dots = row_products(grad_enc_context, enc_context)
    enc_grad_query, enc_grad_keys, enc_grad_values, grad_enc_bias = attend_back(
        enc_qkv[0],
        enc_logs,
        enc_dots,
        grad_enc_context,
        enc_ids,
        enc_lengths,
        "enc",
        enc_table,
        enc_extent,
        lambda folder, initial: folder(
            initial,
            (
                lax.all_gather(enc_qkv[1], "seq", axis=1, tiled=True),
                lax.all_gather(enc_qkv[2], "seq", axis=1, tiled=True),
            ),
            jnp.int32(0),
        ),
    )
    enc_key_grad, enc_value_grad = owned_key_grads(
        enc_qkv[1],
        enc_qkv[2],
        enc_ids,
        enc_lengths,
        "enc",
        enc_table,
        enc_extent,
        lambda folder, initial: folder(
            initial,
            (
                lax.all_gather(enc_qkv[0], "seq", axis=1, tiled=True),
                lax.all_gather(grad_enc_context, "seq", axis=1, tiled=True),
                lax.all_gather(
                    rows_first(enc_logs).astype(jnp.bfloat16), "seq", axis=1, tiled=True
                ).astype(jnp.float32),
                lax.all_gather(
                    rows_first(enc_dots).astype(jnp.bfloat16), "seq", axis=1, tiled=True
                ).astype(jnp.float32),
            ),
            jnp.int32(0),
        ),
    )
    enc_grads = rounded(jnp.stack([enc_grad_query, enc_key_grad, enc_value_grad]))
    grad_in_zero = jnp.einsum(
        "srd,jsre->jde", norm_a_low, enc_grads, preferred_element_type=jnp.float32
    )
    grad_norm_a = jnp.einsum(
        "jsre,jde->srd", enc_grads, full_in[0], preferred_element_type=jnp.float32
    )
    grad_enc_part, grad_gain_zero = rms_back(enc_values, gain_rows[0], grad_norm_a)
    grad_enc_input = grad_enc_mid + grad_enc_part
    grad_cross_in = jnp.concatenate([grad_query_two[None], grad_pair_two], axis=0)
    grad_attention_in = jnp.stack([grad_in_zero, grad_in_one, grad_cross_in])
    grad_attention_out = jnp.stack([grad_out_zero, grad_out_one, grad_out_two])
    grad_hidden_in = jnp.stack([grad_hin_zero, grad_hin_one])
    grad_hidden_out = jnp.stack([grad_hout_zero, grad_hout_one])
    grad_gains = jnp.stack(
        [
            grad_gain_zero,
            grad_gain_one,
            grad_gain_two,
            grad_gain_three,
            grad_gain_four,
            grad_gain_five,
            grad_gain_six,
        ]
    )
    shard_in, shard_out, shard_hin, shard_hout, shard_gains = (
        lax.psum_scatter(grad_attention_in, ("dp", "seq"), scatter_dimension=2, tiled=True),
        lax.psum_scatter(grad_attention_out, ("dp", "seq"), scatter_dimension=1, tiled=True),
        lax.psum_scatter(grad_hidden_in, ("dp", "seq"), scatter_dimension=2, tiled=True),
        lax.psum_scatter(grad_hidden_out, ("dp", "seq"), scatter_dimension=1, tiled=True),
        lax.psum_scatter(grad_gains, ("dp", "seq"), scatter_dimension=1, tiled=True),
    )
    bucket_count = position_bias.shape[1]
    grad_position = jnp.stack(
        [
            bucket_grad(enc_buckets, grad_enc_bias, bucket_count),
            bucket_grad(dec_buckets, grad_dec_bias, bucket_count),
        ]
    )
    squares_in = shard_in * shard_in
    squares_out = shard_out * shard_out
    squares_hin = shard_hin * shard_hin
    squares_hout = shard_hout * shard_hout
    col_in, col_out, col_hin, col_hout, grad_position = lax.psum(
        (
            jnp.sum(squares_in, axis=2),
            jnp.sum(squares_out, axis=1),
            jnp.sum(squares_hin, axis=2),
            jnp.sum(squares_hout, axis=1),
            grad_position,
        ),
        ("dp", "seq"),
    )
    return (
        rounded(memory),
        rounded(dec_final),
        grad_enc_input,
        grad_dec_input,
        shard_in,
        shard_out,
        shard_hin,
        shard_hout,
        shard_gains,
        grad_position,
        0.5 * jnp.mean(squares_in, axis=-1),
        0.5 * col_in / D,
        0.5 * jnp.mean(squares_out, axis=-1),
        0.5 * col_out / D,
        0.5 * jnp.mean(squares_hin, axis=-1),
        0.5 * col_hin / D,
        0.5 * jnp.mean(squares_hout, axis=-1),
        0.5 * col_hout / FF,
    )


WAYS = 4
SETS = HEADS // WAYS
WIDTH = SETS * HEAD
VMEM_LIMIT = 16 * 2**20


def swap(values, axis):
    return lax.ppermute(values, axis, [(0, 1), (1, 0)])


def shift_z(values, hops, count):
    return lax.ppermute(values, "dp", [(i, (i + hops) % count) for i in range(count)])


def pair_up(mine, other, bit):
    first = bit == 0
    return jnp.stack([jnp.where(first, mine, other), jnp.where(first, other, mine)])


def pick(values, index, axis=0):
    return lax.dynamic_index_in_dim(values, index, axis, keepdims=False)


class Place:
    def __init__(self, depth):
        self.depth = depth
        self.z, self.y, self.x, self.c = [lax.axis_index(a) for a in ("dp", "y", "x", "c")]
        self.q = 2 * self.x + self.c
        self.index = (self.z * 2 + self.y) * WAYS + self.q


def exchange_over_x(place, pieces):
    halves = pieces.reshape((2, 2) + pieces.shape[1:])
    got = swap(pick(halves, 1 - place.x), "x")
    return pair_up(pick(halves, place.x), got, place.x)


def exchange_over_cores(place, both):
    got = swap(pick(both, 1 - place.c, 1), "c")
    whole = pair_up(pick(both, place.c, 1), got, place.c)
    return jnp.swapaxes(whole, 0, 1).reshape((4,) + both.shape[2:])


def exchange_columns(place, pieces):
    return exchange_over_cores(place, exchange_over_x(place, pieces))


def along_z(place, piece, *earlier):
    depth = place.depth
    held = jnp.zeros((depth,) + piece.shape, piece.dtype)
    arrivals = [shift_z(piece, k, depth) for k in range(1, depth)]
    if earlier:
        arrivals = [after(block, *earlier) for block in arrivals]
    for hops, block in enumerate([piece] + arrivals):
        held = lax.dynamic_update_index_in_dim(held, block, (place.z - hops) % depth, 0)
    return held


def along_y(place, held):
    other = swap(held, "y")
    first = place.y == 0
    pair = [jnp.where(first, held, other), jnp.where(first, other, held)]
    return jnp.stack(pair, axis=1).reshape(-1, held.shape[-1])


def scatter_y(place, parts):
    parts = parts.reshape((place.depth, 2) + parts.shape[1:])
    sent = swap(pick(parts, 1 - place.y, 1), "y")
    return pick(parts, place.y, 1).astype(F32) + sent.astype(F32)


def scatter_z(place, halves):
    depth = place.depth
    low = rounded(halves)
    total = pick(halves, place.z)
    for hops in range(1, depth):
        sent = shift_z(pick(low, (place.z + hops) % depth), hops, depth)
        total = total + sent.astype(F32)
    return total


def after(values, *earlier):
    return lax.optimization_barrier((values,) + earlier)[0]


def turn(values, depth):
    pairs = []
    for d in range(depth):
        for y in range(2):
            for q in range(WAYS):
                pairs.append((d * 8 + y * 4 + q, q * 8 + y * 4 + d))
    return lax.ppermute(values, ("dp", "y", "x", "c"), pairs)


def matmul(a, b):
    return jnp.dot(a, b, preferred_element_type=jnp.float32)


def matmul_nt(a, b):
    return lax.dot_general(a, b, (((1,), (1,)), ((), ())), preferred_element_type=jnp.float32)


def matmul_tn(a, b):
    return lax.dot_general(a, b, (((0,), (0,)), ((), ())), preferred_element_type=jnp.float32)


def call(kernel, name, outs, args, micros, scratch=()):
    whole = pl.BlockSpec(memory_space=pltpu.VMEM)
    arrays = [a[0] if isinstance(a, tuple) else a for a in args]
    specs = [a[1] if isinstance(a, tuple) else whole for a in args]
    late = [k for k, spec in enumerate(specs) if spec is LATE]
    plain = (whole, SCALARS, LATE, ANYWHERE)
    windows = any(all(spec is not p for p in plain) for spec in specs)
    shapes = tuple(jax.ShapeDtypeStruct(s, t) for s, t in outs)
    moved = sum(a.size * a.dtype.itemsize for a in list(arrays) + list(shapes))
    buffers = [pltpu.VMEM(arrays[k].shape, arrays[k].dtype) for k in late]

    def bring_in(*refs):
        if not late:
            return kernel(*refs)
        refs, places, semaphores = list(refs[: -len(late) - 1]), refs[-len(late) - 1 : -1], refs[-1]
        copies = [
            pltpu.make_async_copy(refs[k], place, semaphores.at[n])
            for n, (k, place) in enumerate(zip(late, places))
        ]
        for copy in copies:
            copy.start()
        for copy in copies:
            copy.wait()
        for k, place in zip(late, places):
            refs[k] = place
        return kernel(*refs)

    if late:
        buffers.append(pltpu.SemaphoreType.DMA((len(late),)))
    return pl.pallas_call(
        bring_in,
        grid=(1,) if windows else (),
        out_shape=shapes,
        in_specs=specs,
        out_specs=(whole,) * len(shapes),
        scratch_shapes=list(scratch) + buffers,
        compiler_params=pltpu.CompilerParams(vmem_limit_bytes=VMEM_LIMIT),
        cost_estimate=pl.CostEstimate(
            flops=int(micros * 1e7), bytes_accessed=moved // 32, transcendentals=0
        ),
        name=name,
    )(*arrays)


LATE = pl.BlockSpec(memory_space=pltpu.HBM)
ANYWHERE = pl.BlockSpec(memory_space=pl.ANY)
SCALARS = pl.BlockSpec(memory_space=pltpu.SMEM)
BF, F32 = jnp.bfloat16, jnp.float32


def column_block(array, index):
    rows, columns = array.shape
    return (array, pl.BlockSpec((rows, 2 * WIDTH), lambda _: (0, index)))


def norm_rows(values, gain):
    return values * lax.rsqrt(jnp.mean(values * values, axis=-1, keepdims=True) + EPSILON) * gain


def norm_back(values, gain, upstream):
    scale = lax.rsqrt(jnp.mean(values * values, axis=-1, keepdims=True) + EPSILON)
    unit = values * scale
    inner = upstream * gain
    grad = scale * (inner - unit * jnp.mean(inner * unit, axis=-1, keepdims=True))
    return grad, jnp.sum(upstream * unit, axis=0, keepdims=True)


def self_kernel(gain, q_at, x_ref, gains_ref, kva_ref, qa_ref, kvb_ref, qb_ref, *outs):
    n_ref, q_ref, kv_ref = outs
    n = norm_rows(x_ref[...].astype(F32), gains_ref[gain : gain + 1, :]).astype(BF)
    n_ref[...] = n
    for e, (kv, q) in enumerate(((kva_ref, qa_ref), (kvb_ref, qb_ref))):
        kv_ref[e] = matmul(n, kv[:, : 2 * WIDTH]).astype(BF)
        q_ref[e] = matmul(n, q[:, q_at : q_at + WIDTH]).astype(BF)


def self_project(x, gains, gain, kv_own, q_own, kv_sib, q_sib, q_at, name):
    rows = x.shape[0]
    return call(
        functools.partial(self_kernel, gain, q_at),
        name,
        [((rows, D), BF), ((2, rows, WIDTH), BF), ((2, rows, 2 * WIDTH), BF)],
        [x, gains, kv_own, q_own, kv_sib, q_sib],
        2.5,
    )


def memory_kernel(res_ref, part_ref, got_ref, gains_ref, kva_ref, kvb_ref, *outs):
    last_ref, low_ref, kv_ref = outs
    last = res_ref[...].astype(F32) + part_ref[...] + got_ref[...].astype(F32)
    last_ref[...] = last
    low = norm_rows(last, gains_ref[2:3, :]).astype(BF)
    low_ref[...] = low
    for e, kv in enumerate((kva_ref, kvb_ref)):
        kv_ref[e] = matmul(low, kv[...]).astype(BF)


def cross_kernel(q_at, res_ref, part_ref, got_ref, gains_ref, qa_ref, qb_ref, *outs):
    mid_ref, low_ref, q_ref = outs
    mid = res_ref[...].astype(F32) + part_ref[...] + got_ref[...].astype(F32)
    mid_ref[...] = mid
    low = norm_rows(mid, gains_ref[4:5, :]).astype(BF)
    low_ref[...] = low
    for e, q in enumerate((qa_ref, qb_ref)):
        q_ref[e] = matmul(low, q[:, q_at : q_at + WIDTH]).astype(BF)


def lay_out_keys(core, kv_ref, got_ref, keys):
    block = kv_ref.shape[1] // 4
    for e in range(2):
        for k in range(4):
            at = pl.multiple_of(block * (2 * k + core), block)
            keys[e, pl.ds(at, block), :] = kv_ref[e, k * block : (k + 1) * block, :]
            at = pl.multiple_of(block * (2 * k + 1 - core), block)
            keys[e, pl.ds(at, block), :] = got_ref[1 - e, k * block : (k + 1) * block, :]


def attend_kernel(causal, biased, *refs):
    if biased:
        scalars, q_ref, kv_ref, got_ref, table_ref, oa_ref, ob_ref = refs[:7]
    else:
        scalars, q_ref, kv_ref, got_ref, oa_ref, ob_ref = refs[:6]
    ctx_ref, p_ref, part_ref, low_ref, keys = refs[-5:]
    core, length = scalars[0], scalars[1]
    lay_out_keys(core, kv_ref, got_ref, keys)
    rows, extent = q_ref.shape[1], keys.shape[1]
    block = rows // 4
    cols = lax.broadcasted_iota(jnp.int32, (block, extent), 1)
    ids = lax.broadcasted_iota(jnp.int32, (block, extent), 0)
    total = None
    for e in range(2):
        for h in range(SETS):
            at = slice(h * HEAD, (h + 1) * HEAD)
            k = keys[e, :, at]
            v = keys[e, :, WIDTH + h * HEAD : WIDTH + (h + 1) * HEAD]
            scores = matmul_nt(q_ref[e, :, at], k)
            if biased:
                line = table_ref[e * SETS + h : e * SETS + h + 1, :]
                skew = pltpu.roll(
                    jnp.broadcast_to(line, (block, 2 * extent)),
                    2 * extent - (block - 1),
                    1,
                    stride=1,
                    stride_axis=0,
                )
            for i in range(4):
                here = slice(i * block, (i + 1) * block)
                s = scores[here] * (HEAD**-0.5)
                if biased:
                    begin = (3 - i) * 2 * block
                    s = s + skew[:, begin : begin + extent]
                visible = cols < length
                if causal:
                    visible = visible & (cols <= ids + (i * 2 * block + core * block))
                s = jnp.where(visible, s, NEGATIVE)
                weights = jnp.exp(s - jnp.max(s, axis=-1, keepdims=True))
                weights = weights * (1.0 / jnp.sum(weights, axis=-1, keepdims=True))
                p_ref[e * SETS + h, here, :] = weights.astype(BF)
            ctx_ref[e, :, at] = matmul(p_ref[e * SETS + h], v)
        term = matmul(ctx_ref[e].astype(BF), (oa_ref, ob_ref)[e][...])
        total = term if total is None else total + term
    part_ref[...] = total
    low_ref[...] = total.astype(BF)


def attend_local(scalars, q, kv, got, table, out_own, out_sib, causal, name):
    rows = q.shape[1]
    extent = 2 * rows
    args = [(scalars, SCALARS), q, kv, got] + ([] if table is None else [table])
    return call(
        functools.partial(attend_kernel, causal, table is not None),
        name,
        [
            ((2, rows, WIDTH), F32),
            ((2 * SETS, rows, extent), BF),
            ((rows, D), F32),
            ((rows, D), BF),
        ],
        args + [out_own, out_sib],
        5.5,
        [pltpu.VMEM((2, extent, 2 * WIDTH), BF)],
    )


def unpack_into(w_ref, columns, down):
    blocks, rows = 8, down.shape[0] // 8
    half, third = rows // 2, down.shape[1] // 3
    step = rows + half
    for b in range(blocks):
        down[b * rows : (b + 1) * rows, : 2 * third] = w_ref[
            b * step : b * step + rows, columns : columns + 2 * third
        ]
        for k in range(2):
            down[b * rows + k * half : b * rows + (k + 1) * half, 2 * third :] = w_ref[
                b * step + rows : (b + 1) * step,
                columns + k * third : columns + (k + 1) * third,
            ]


GELU_A, GELU_B = (2 / math.pi) ** 0.5, 0.044715


def gelu_tanh(gate):
    return jnp.tanh(GELU_A * (gate + GELU_B * gate * gate * gate))


def ffn_kernel(gain, res_ref, part_ref, got_ref, gains_ref, wa_ref, wb_ref, *refs):
    mid_ref, n_ref, gu_ref, hid_ref, out_ref, low_ref, down = refs
    mid = res_ref[...].astype(F32) + part_ref[...] + got_ref[...].astype(F32)
    mid_ref[...] = mid
    n = norm_rows(mid, gains_ref[gain : gain + 1, :]).astype(BF)
    n_ref[...] = n
    units = down.shape[0]
    total = None
    for e, w_ref in enumerate((wa_ref, wb_ref)):
        gu_ref[e] = matmul(n, w_ref[:, : 2 * units])
        gate, up = gu_ref[e, :, :units], gu_ref[e, :, units:]
        hid_ref[e] = (0.5 * gate * (1.0 + gelu_tanh(gate)) * up).astype(BF)
        unpack_into(w_ref, 2 * units, down)
        term = matmul(hid_ref[e], down[...])
        total = term if total is None else total + term
    out_ref[...] = total
    low_ref[...] = total.astype(BF)


def ffn_local(res, part, got, gains, gain, w_own, w_sib, units, name):
    rows = res.shape[0]
    return call(
        functools.partial(ffn_kernel, gain),
        name,
        [
            ((rows, D), F32),
            ((rows, D), BF),
            ((2, rows, 2 * units), F32),
            ((2, rows, units), BF),
            ((rows, D), F32),
            ((rows, D), BF),
        ],
        [res, part, got, gains, w_own, w_sib],
        3.0,
        [pltpu.VMEM((units, D), BF)],
    )


def ffn_back_kernel(decoder, val_ref, part_ref, got_ref, cot_ref, gains_ref, *refs):
    gu_ref, wa_ref, wb_ref = refs[:3]
    down = refs[-1]
    sent = part_ref[...] + got_ref[...].astype(F32)
    if decoder:
        final_ref, g_ref, dgain_ref, low_ref, dgu_ref, out_ref, out_low_ref = refs[3:-1]
        gain = gains_ref[6:7, :]
        values = val_ref[...] + sent
        upstream = cot_ref[...].astype(F32)
        final_ref[...] = norm_rows(values, gain).astype(BF)
    else:
        g_ref, dgain_ref, low_ref, dgu_ref, out_ref, out_low_ref = refs[3:-1]
        gain = gains_ref[2:3, :]
        values = val_ref[...]
        upstream = cot_ref[...].astype(F32) + sent
    grad, dgain_ref[...] = norm_back(values, gain, upstream)
    g_ref[...] = grad
    low = grad.astype(BF)
    low_ref[...] = low
    units = down.shape[0]
    total = None
    for e, w_ref in enumerate((wa_ref, wb_ref)):
        unpack_into(w_ref, 2 * units, down)
        grad_hidden = matmul_nt(low, down[...])
        gate, up = gu_ref[e, :, :units], gu_ref[e, :, units:]
        t = gelu_tanh(gate)
        slope = 0.5 * (1.0 + t) + 0.5 * gate * (1.0 - t * t) * GELU_A * (
            1.0 + 3.0 * GELU_B * gate * gate
        )
        dgu_ref[e, :, :units] = (grad_hidden * up * slope).astype(BF)
        dgu_ref[e, :, units:] = (grad_hidden * (0.5 * gate * (1.0 + t))).astype(BF)
        term = matmul_nt(dgu_ref[e], w_ref[:, : 2 * units])
        total = term if total is None else total + term
    out_ref[...] = total
    out_low_ref[...] = total.astype(BF)


def ffn_back(decoder, values, part, got, cot, gains, gate_up, w_own, w_sib, name):
    rows, units = values.shape[0], gate_up.shape[2] // 2
    outs = [((rows, D), BF)] if decoder else []
    outs += [
        ((rows, D), F32),
        ((1, D), F32),
        ((rows, D), BF),
        ((2, rows, 2 * units), BF),
        ((rows, D), F32),
        ((rows, D), BF),
    ]
    return call(
        functools.partial(ffn_back_kernel, decoder),
        name,
        outs,
        [values, part, got, cot, gains, gate_up, w_own, w_sib],
        4.0,
        [pltpu.VMEM((units, D), BF)],
    )


def ffn_weights_kernel(n_ref, dgu_ref, hid_ref, low_ref, own_ref, sib_ref):
    units = hid_ref.shape[2]
    rows, half, third = units // 8, units // 16, D // 3
    step = rows + half
    for e, out in enumerate((own_ref, sib_ref)):
        out[:, : 2 * units] = matmul_tn(n_ref[...], dgu_ref[e]).astype(BF)
        down = matmul_tn(hid_ref[e], low_ref[...]).astype(BF)
        for b in range(8):
            out[b * step : b * step + rows, 2 * units :] = down[
                b * rows : (b + 1) * rows, : 2 * third
            ]
            for k in range(2):
                out[
                    b * step + rows : (b + 1) * step,
                    2 * units + k * third : 2 * units + (k + 1) * third,
                ] = down[b * rows + k * half : b * rows + (k + 1) * half, 2 * third :]


def ffn_weights(n, dgu, hid, low, name):
    units = hid.shape[2]
    shape = ((D, 2 * units + 2 * D // 3), BF)
    return call(
        ffn_weights_kernel, name, [shape, shape], [n, dgu, hid, low], 1.5
    )


def attend_back_kernel(gain, biased, scalars, up_ref, val_ref, part_ref, got_ref, *refs):
    gains_ref, oa_ref, ob_ref, q_ref, kv_ref, kvgot_ref, p_ref, ctx_ref = refs[:8]
    g_ref, dgain_ref, low_ref, dq_ref, mine_ref, other_ref = refs[8:14]
    keys, dkeys, ds_ref = refs[-3:]
    core = scalars[0]
    grad, dgain_ref[...] = norm_back(
        val_ref[...], gains_ref[gain : gain + 1, :], part_ref[...] + got_ref[...].astype(F32)
    )
    grad = up_ref[...] + grad
    g_ref[...] = grad
    low = grad.astype(BF)
    low_ref[...] = low
    lay_out_keys(core, kv_ref, kvgot_ref, keys)
    rows, extent = q_ref.shape[1], keys.shape[1]
    block = rows // 4
    factor = HEAD**-0.5
    for e in range(2):
        g = matmul_nt(low, (oa_ref, ob_ref)[e][...]).astype(BF)
        products = g.astype(F32) * ctx_ref[e]
        for h in range(SETS):
            at = slice(h * HEAD, (h + 1) * HEAD)
            k = keys[e, :, at]
            v = keys[e, :, WIDTH + h * HEAD : WIDTH + (h + 1) * HEAD]
            dots = jnp.sum(products[:, at], axis=-1, keepdims=True)
            dp = matmul_nt(g[:, at], v)
            sums = [None] * 7
            for i in range(4):
                here = slice(i * block, (i + 1) * block)
                ds = p_ref[e * SETS + h, here, :].astype(F32) * (dp[here] - dots[here])
                if biased:
                    for j in range(4):
                        part = ds[:, j * 2 * block : (j + 1) * 2 * block]
                        slot = 3 - i + j
                        sums[slot] = part if sums[slot] is None else sums[slot] + part
                ds_ref[here, :] = (ds * factor).astype(BF)
            dq_ref[e, :, at] = matmul(ds_ref[...], k).astype(BF)
            dkeys[:, at] = matmul_tn(ds_ref[...], q_ref[e, :, at])
            dkeys[:, WIDTH + h * HEAD : WIDTH + (h + 1) * HEAD] = matmul_tn(
                p_ref[e * SETS + h], g[:, at]
            )
            if biased:
                dtable_ref = refs[14]
                band = jnp.concatenate(sums + [jnp.zeros_like(sums[0])], axis=1)
                ids = lax.broadcasted_iota(jnp.int32, band.shape, 0)
                bit = 1
                while bit < block:
                    moved = pltpu.roll(band, 2 * extent - bit, 1)
                    band = jnp.where((ids & bit) != 0, moved, band)
                    bit *= 2
                line = jnp.sum(band, axis=0, keepdims=True)
                dtable_ref[e * SETS + h : e * SETS + h + 1, :] = pltpu.roll(line, block - 1, 1)
        for k in range(4):
            at = pl.multiple_of(block * (2 * k + core), block)
            mine_ref[e, k * block : (k + 1) * block, :] = dkeys[pl.ds(at, block), :]
            at = pl.multiple_of(block * (2 * k + 1 - core), block)
            other_ref[1 - e, k * block : (k + 1) * block, :] = dkeys[
                pl.ds(at, block), :
            ].astype(BF)


def attend_local_back(gain, biased, scalars, upstream, values, part, got, gains, *rest, name):
    rows, extent = upstream.shape[0], 2 * upstream.shape[0]
    outs = [
        ((rows, D), F32),
        ((1, D), F32),
        ((rows, D), BF),
        ((2, rows, WIDTH), BF),
        ((2, rows, 2 * WIDTH), F32),
        ((2, rows, 2 * WIDTH), BF),
    ]
    if biased:
        outs.append(((2 * SETS, 2 * extent), F32))
    return call(
        functools.partial(attend_back_kernel, gain, biased),
        name,
        outs,
        [(scalars, SCALARS), (upstream, LATE), (values, LATE), part, got, gains]
        + list(rest[:2])
        + [(a, LATE) for a in rest[2:]],
        9.0 if biased else 6.0,
        [
            pltpu.VMEM((2, extent, 2 * WIDTH), BF),
            pltpu.VMEM((extent, 2 * WIDTH), F32),
            pltpu.VMEM((rows, extent), BF),
        ],
    )


def project_back_kernel(split, q_at, dq_ref, mine_ref, got_ref, *refs):
    kva_ref, qa_ref, kvb_ref, qb_ref = refs[:4]
    dkv_ref = refs[4]
    from_keys = from_queries = None
    for e, (kv, q) in enumerate(((kva_ref, qa_ref), (kvb_ref, qb_ref))):
        dkv = (mine_ref[e] + got_ref[e].astype(F32)).astype(BF)
        dkv_ref[e] = dkv
        term = matmul_nt(dkv, kv[:, : 2 * WIDTH])
        from_keys = term if e == 0 else from_keys + term
        term = matmul_nt(dq_ref[e], q[:, q_at : q_at + WIDTH])
        from_queries = term if e == 0 else from_queries + term
    outs = [from_keys, from_queries] if split else [from_keys + from_queries]
    for k, total in enumerate(outs):
        refs[5 + 2 * k][...] = total
        refs[6 + 2 * k][...] = total.astype(BF)


def project_back(split, dq, mine, got, kv_own, q_own, kv_sib, q_sib, q_at, name):
    rows = dq.shape[1]
    outs = [((2, rows, 2 * WIDTH), BF)] + [((rows, D), F32), ((rows, D), BF)] * (1 + split)
    return call(
        functools.partial(project_back_kernel, split, q_at),
        name,
        outs,
        [dq, mine, got, kv_own, q_own, kv_sib, q_sib],
        2.5,
    )


def attend_weights_kernel(count, *refs):
    ins, (own_ref, sib_ref, out_own_ref, out_sib_ref) = refs[:-4], refs[-4:]
    for k in range(count):
        nq_ref, nkv_ref, dq_ref, dkv_ref, ctx_ref, low_ref = ins[6 * k : 6 * k + 6]
        kv_at, q_at = 2 * WIDTH * k, 2 * WIDTH * count + WIDTH * k
        for e, (in_ref, out_ref) in enumerate(((own_ref, out_own_ref), (sib_ref, out_sib_ref))):
            if k == 0 and in_ref.shape[1] > 3 * count * WIDTH:
                in_ref[...] = jnp.zeros_like(in_ref)
            in_ref[:, kv_at : kv_at + 2 * WIDTH] = matmul_tn(nkv_ref[...], dkv_ref[e]).astype(BF)
            in_ref[:, q_at : q_at + WIDTH] = matmul_tn(nq_ref[...], dq_ref[e]).astype(BF)
            out_ref[k] = matmul_tn(ctx_ref[e].astype(BF), low_ref[...]).astype(BF)


def attend_weights(name, *attentions):
    count, rows = len(attentions), attentions[0][0].shape[0]
    inner, outer = ((D, -(-3 * count * WIDTH // 128) * 128), BF), ((count, WIDTH, D), BF)
    own, sib, out_own, out_sib = call(
        functools.partial(attend_weights_kernel, count),
        name,
        [inner, inner, outer, outer],
        [a for attention in attentions for a in attention],
        1.0 * count,
    )
    return own, out_own, sib, out_sib


IN_ORDER = (8, 6, 7, 4, 0, 1, 5, 2, 3)


def sums_kernel(own, late_ref, dec_ref, self_ref, out_ref):
    inner, third, half = 6 * WIDTH, D // 3, D // 2
    width = dec_ref.shape[1]
    wide, rows = width - 2 * third, dec_ref.shape[0] * 2 // 3
    out_ref[...] = jnp.zeros_like(out_ref)

    def squares(values, rows_in_all):
        values = values.astype(F32)
        return values * values * (0.5 / rows_in_all)

    def line(values):
        return jnp.sum(values, axis=0, keepdims=True)

    def put(at, values):
        for k in range(0, values.shape[1], 128):
            size = min(128, values.shape[1] - k)
            out_ref[at + k // 128 : at + k // 128 + 1, :size] = values[:, k : k + size]

    put(0, line(squares(late_ref[:, :wide], D)))
    put(wide // 128, line(squares(dec_ref[:, :wide], D)))
    at = 2 * wide // 128
    put(at, line(squares(late_ref[:, width : width + inner], D)))
    put(at + inner // 128, line(squares(self_ref[:, third : third + 3 * WIDTH], D)))
    at = 30
    for ref in (late_ref, dec_ref):
        down = squares(ref[:, wide:width], FF)
        put(at, line(down[:rows]))
        put(at + 2 * third // 128, line(down[rows:, :third]) + line(down[rows:, third:]))
        at += D // 128
    outer = squares(self_ref[:, :third], D)
    for k in range(3):
        put(at + k * third // 128, line(outer[k * own : (k + 1) * own]))
    at += D // 128
    outer = squares(late_ref[:, width + inner :], D)
    for k in range(2):
        for side in range(2):
            begin = (2 * side + k) * own
            put(at + side * half // 128, line(outer[begin : begin + own]))
        at += D // 128


def hold_kernel(values_ref, earlier_ref, out_ref):
    out_ref[...] = values_ref[...]


def half_mean_rows(values):
    ones = jnp.full((8, values.shape[1]), 0.5 / values.shape[1], F32)
    sums = lax.dot_general(
        ones,
        values * values,
        (((1,), (1,)), ((), ())),
        precision=HIGHEST,
        preferred_element_type=F32,
    )
    return sums[:1]


def shards_kernel(ff_own, columns_ref, turned_ref, late_ref, dec_ref, *outs):
    in_ref, out_ref, hin_ref, hout_ref, row_in_ref, row_out_ref, row_hin_ref, row_hout_ref = outs
    third = D // 3
    width = dec_ref.shape[1]
    wide = width - 2 * third
    units = wide // 2
    for k, at in enumerate(IN_ORDER):
        at = wide + at * WIDTH
        for q in range(WAYS):
            piece = columns_ref[q, :, at : at + WIDTH]
            in_ref[k // 3, k % 3, :, q * WIDTH : (q + 1) * WIDTH] = piece
        row_in_ref[k : k + 1, :] = half_mean_rows(in_ref[k // 3, k % 3])
    out_ref[...] = turned_ref[...]
    for k in range(3):
        row_out_ref[k : k + 1, :] = half_mean_rows(turned_ref[k])
    for layer in range(2):
        begin = wide + 9 * WIDTH if layer == 0 else 0
        for j in range(2):
            for k in range(units // ff_own):
                first = begin + j * units + k * ff_own
                for q in range(WAYS):
                    at = (WAYS * k + q) * ff_own
                    piece = columns_ref[q, :, first : first + ff_own]
                    hin_ref[layer, j, :, at : at + ff_own] = piece
            row_hin_ref[2 * layer + j : 2 * layer + j + 1, :] = half_mean_rows(hin_ref[layer, j])
    for layer, ref in enumerate((late_ref, dec_ref)):
        down = ref[:, wide:width].astype(F32)
        hout_ref[layer, :, : 2 * third] = down[:ff_own]
        half = ff_own // 2
        hout_ref[layer, :half, 2 * third :] = down[ff_own:, :third]
        hout_ref[layer, half:, 2 * third :] = down[ff_own:, third:]
        row_hout_ref[layer : layer + 1, :] = half_mean_rows(hout_ref[layer])


def input_kernel(gain, up_ref, x_ref, part_ref, got_ref, gains_ref, out_ref, dgain_ref):
    grad, dgain_ref[...] = norm_back(
        x_ref[...].astype(F32),
        gains_ref[gain : gain + 1, :],
        part_ref[...] + got_ref[...].astype(F32),
    )
    out_ref[...] = up_ref[...] + grad


def input_back(gain, upstream, x, part, got, gains, name):
    return call(
        functools.partial(input_kernel, gain),
        name,
        [(upstream.shape, F32), ((1, D), F32)],
        [upstream, x, part, got, gains],
        1.5,
    )


def gather_own_rows(place, mine, other_seq):
    near = pair_up(mine, swap(other_seq, "y"), place.y)
    far = pair_up(near, swap(near, "x"), place.x)
    far = far.transpose(2, 1, 0, 3, 4)
    return far.reshape(far.shape[0], -1, far.shape[4])


def give_back(place, half):
    blocks = half.reshape(2, 2, -1, half.shape[1])
    blocks = pick(blocks, place.x, 1)
    other = swap(pick(blocks, 1 - place.y), "y")
    return pair_up(pick(blocks, place.y), other, place.y)


def sum_everywhere(place, values):
    depth = place.depth
    for axis in ("c", "x", "y"):
        values = values + swap(values, axis)
    return values + sum(shift_z(values, k, depth) for k in range(1, depth))


def pack_down(rows):
    half, third = rows.shape[-2] // 2, rows.shape[-1] // 3
    last = rows[..., 2 * third :]
    last = jnp.concatenate([last[..., :half, :], last[..., half:, :]], axis=-1)
    return jnp.concatenate([rows[..., : 2 * third], last], axis=-2)


def unpack_down(packed):
    half, third = packed.shape[-2] // 3, packed.shape[-1] // 2
    last = packed[..., 2 * half :, :]
    last = jnp.concatenate([last[..., :third], last[..., third:]], axis=-2)
    return jnp.concatenate([packed[..., : 2 * half, :], last], axis=-1)


def pack_out(pair):
    rows = pair.reshape(pair.shape[:-3] + (-1, pair.shape[-1]))
    half = rows.shape[-1] // 2
    return jnp.concatenate([rows[..., :half], rows[..., half:]], axis=-2)


def unpack_out_piece(packed):
    half = packed.shape[-2] // 2
    rows = jnp.concatenate([packed[..., :half, :], packed[..., half:, :]], axis=-1)
    return rows.reshape(rows.shape[:-2] + (2, half // 2, rows.shape[-1]))


def unpack_out(packed, depth):
    pair = unpack_out_piece(packed)
    pair = pair.reshape((depth, 2) + pair.shape[1:])
    pair = pair.transpose(2, 1, 0, 3, 4)
    return pair.reshape(2, -1, pair.shape[-1])


def turned_parts(grads, depth):
    parts = grads.reshape(2, depth, -1, grads.shape[1]).transpose(1, 0, 2, 3)
    return parts.reshape(2 * depth, -1, grads.shape[1])


def grouped(
    depth,
    enc_input,
    dec_input,
    enc_lengths,
    dec_lengths,
    enc_buckets,
    dec_buckets,
    attention_in,
    attention_out,
    hidden_in,
    hidden_out,
    norm_gains,
    position_bias,
    enc_cotangent,
    dec_cotangent,
):
    place = Place(depth)
    y, q = place.y, place.q
    block = enc_input.shape[1]
    length = block * 8
    own = attention_in.shape[2]
    ff_own = hidden_out.shape[1]
    units = ff_own * 2 * depth
    group = WAYS * own

    pieces = attention_in.reshape(3, 3, own, WAYS, WIDTH).transpose(3, 0, 1, 2, 4)
    queries, keys, values = pieces[:, :, 0], pieces[:, :, 1], pieces[:, :, 2]
    gain_piece = jnp.pad(norm_gains.T, ((0, 0), (0, 64 - norm_gains.shape[0])))
    gain_piece = jnp.broadcast_to(gain_piece[None], (WAYS,) + gain_piece.shape)
    turned = turn(attention_out, depth)
    hidden_pieces = hidden_in.reshape(2, 2, own, 2 * depth, WAYS, ff_own)
    hidden_pieces = hidden_pieces.transpose(4, 0, 2, 1, 3, 5).reshape(WAYS, 2, own, 2 * units)
    blocks_in = [keys[:, 0], values[:, 0], queries[:, 0], gain_piece]
    blocks_in += [keys[:, 1], values[:, 1], keys[:, 2], values[:, 2], queries[:, 1], queries[:, 2]]
    blocks_in += [hidden_pieces[:, 0], hidden_pieces[:, 1]]
    everything = exchange_columns(place, jnp.concatenate(blocks_in, axis=2)).reshape(group, -1)
    cuts = [3 * WIDTH + 64, 9 * WIDTH + 64, 9 * WIDTH + 64 + 2 * units]
    enc_piece, rest, ffn_enc, ffn_dec = jnp.split(everything, cuts, axis=1)
    third = turned[0].reshape(own, 3, D // 3).transpose(1, 0, 2).reshape(3 * own, D // 3)
    third = jnp.pad(third, ((0, group - 3 * own), (0, 0)))
    enc_piece = jnp.concatenate([enc_piece, third], axis=1)
    rest = jnp.concatenate([rest, pack_out(turned[1:])], axis=1)
    ffn_enc = jnp.concatenate([ffn_enc, pack_down(hidden_out[0])], axis=1)
    ffn_dec = jnp.concatenate([ffn_dec, pack_down(hidden_out[1])], axis=1)

    line = along_z(place, enc_piece)
    w_enc = along_y(place, line)
    w_enc_sib = swap(w_enc, "c")

    def out_rows(whole):
        rows = whole[:, 3 * WIDTH + 64 :].reshape(depth, 2, group, D // 3)[:, :, : 3 * own]
        rows = rows.reshape(depth, 2, 3, own, D // 3).transpose(1, 0, 3, 2, 4)
        return rows.reshape(WIDTH, D)

    def gather(piece):
        return lax.all_gather(piece, ("dp", "y"), axis=0, tiled=True)

    first = gather(jnp.concatenate([rest, ffn_enc], axis=1))
    out_enc, out_enc_sib = out_rows(w_enc), out_rows(w_enc_sib)
    gains = w_enc[:, 3 * WIDTH : 3 * WIDTH + norm_gains.shape[0]].astype(F32).T

    w_self = [w_enc, w_enc, w_enc_sib, w_enc_sib]

    def own_rows(*arrays):
        mine = jnp.stack([pick(a, y) for a in arrays])
        other = jnp.stack([pick(a, 1 - y) for a in arrays])
        return gather_own_rows(place, mine, other)

    enc_rows, dec_rows, *cots = own_rows(enc_input, dec_input, dec_cotangent, enc_cotangent)
    enc_scalars = jnp.stack([place.c, pick(enc_lengths, y)]).astype(jnp.int32)
    dec_scalars = jnp.stack([place.c, pick(dec_lengths, y)]).astype(jnp.int32)

    def head_rows(table):
        mine = lax.dynamic_slice_in_dim(table, q * SETS, SETS, 0)
        theirs = lax.dynamic_slice_in_dim(table, (q + 1 - 2 * place.c) * SETS, SETS, 0)
        table = jnp.concatenate([mine, theirs])
        table = jnp.pad(table, ((0, 0), (0, block)))
        return lax.dynamic_slice_in_dim(table, block * (1 - place.c), 2 * length, 1)

    enc_table = offset_table(enc_buckets, position_bias[0])
    enc_table = head_rows(jnp.pad(enc_table, ((0, 0), (0, 1))))
    dec_table = offset_table(dec_buckets, position_bias[1])
    dec_table = jnp.concatenate(
        [dec_table[:, ::-1], jnp.broadcast_to(dec_table[:, :1], (HEADS, length))], axis=1
    )
    dec_table = head_rows(dec_table)

    n_a, q_enc, kv_enc = self_project(enc_rows, gains, 0, *w_self, 2 * WIDTH, "enc_project")
    kv_enc_got = swap(kv_enc, "c")
    ctx_enc, p_enc, part, low = attend_local(
        enc_scalars, q_enc, kv_enc, kv_enc_got, enc_table, out_enc, out_enc_sib, False, "enc_attend"
    )
    low_enc, part_enc = low, part
    ffn_dec = gather(after(ffn_dec, low_enc))
    got_enc = swap(low_enc, "x")
    first = after(first, got_enc)
    first_sib = swap(first, "c")
    rest, rest_sib = first[:, : ffn_enc.shape[1]], first_sib[:, : ffn_enc.shape[1]]

    out_rest = unpack_out(rest[:, 6 * WIDTH :].reshape(2 * depth, group, -1), depth)
    out_rest_sib = unpack_out(rest_sib[:, 6 * WIDTH :].reshape(2 * depth, group, -1), depth)
    w_dec = [column_block(w, k) for w in (first, first_sib) for k in (0, 2)]
    w_cross = [column_block(w, k) for w in (first, first_sib) for k in (1, 2)]
    ffn_width = ffn_enc.shape[1]
    ffn_enc, ffn_enc_sib = [
        (w, pl.BlockSpec((D, ffn_width), lambda _: (0, 1))) for w in (first, first_sib)
    ]
    out_dec, out_cross = [[(w, pl.BlockSpec((None, WIDTH, D), f)) for w in (out_rest, out_rest_sib)]
        for f in (lambda _: (0, 0, 0), lambda _: (1, 0, 0))]

    n_b, q_dec, kv_dec = self_project(dec_rows, gains, 3, *w_dec, 0, "dec_project")
    kv_dec_got = swap(kv_dec, "c")
    ctx_dec, p_dec, part_dec, low_dec = attend_local(
        dec_scalars, q_dec, kv_dec, kv_dec_got, dec_table, *out_dec, True, "dec_attend"
    )

    enc_mid, n_1, gu_enc, hid_enc, part, low = ffn_local(
        enc_rows, part_enc, after(got_enc, low_dec), gains, 1, ffn_enc, ffn_enc_sib, units, "enc_ffn"
    )
    rows = enc_rows.shape[0]
    dec_mid, n_c, q_cross = call(
        functools.partial(cross_kernel, WIDTH),
        "cross_project",
        [((rows, D), F32), ((rows, D), BF), ((2, rows, WIDTH), BF)],
        [dec_rows, part_dec, swap(low_dec, "x"), gains, w_cross[1], w_cross[3]],
        2.0,
    )
    enc_last, memory_low, kv_cross = call(
        memory_kernel,
        "memory",
        [((rows, D), F32), ((rows, D), BF), ((2, rows, 2 * WIDTH), BF)],
        [enc_mid, part, after(swap(low, "x"), q_cross), gains, w_cross[0], w_cross[2]],
        2.0,
    )
    kv_cross_got = swap(kv_cross, "c")

    ctx_cross, p_cross, part, low = attend_local(
        enc_scalars, q_cross, kv_cross, kv_cross_got, None, *out_cross, False, "cross_attend"
    )
    ffn_dec = after(ffn_dec, low)
    ffn_dec_sib = swap(ffn_dec, "c")
    dec_cross, n_5, gu_dec, hid_dec, part, low = ffn_local(
        dec_mid, part, swap(low, "x"), gains, 5, ffn_dec, ffn_dec_sib, units, "dec_ffn"
    )

    def both(own_grads, sib_grads):
        return (own_grads.astype(F32) + swap(sib_grads, "c").astype(F32)).astype(BF)

    def blocks(grads):
        return grads.reshape(2 * depth, -1, grads.shape[1])

    def scatter(grads):
        return lax.psum_scatter(grads, ("dp", "y"), scatter_dimension=0, tiled=False)

    dec_final, g, gg6, low_d, dgu_dec, part, low = ffn_back(
        True, dec_cross, part, swap(low, "x"), cots[0], gains, gu_dec, ffn_dec, ffn_dec_sib, "dec_ffn_back"
    )
    d_ffn_dec = ffn_weights(n_5, dgu_dec, hid_dec, low_d, "dec_ffn_weights")
    d_ffn_dec = both(*d_ffn_dec)
    got_f = after(swap(low, "x"), d_ffn_dec)
    got = got_f
    g, gg5, low_x, dq_cross, mine, other = attend_local_back(
        5,
        False,
        enc_scalars,
        g,
        dec_cross,
        part,
        got,
        gains,
        *out_cross,
        q_cross,
        kv_cross,
        kv_cross_got,
        p_cross,
        ctx_cross,
        name="cross_attend_back",
    )
    got = swap(other, "c")
    d_ffn_dec = scatter(after(blocks(d_ffn_dec), got_f))
    dkv_cross, part_m, low_m, part_c, low_c = project_back(
        True, dq_cross, mine, got, *w_cross, WIDTH, "cross_project_back"
    )
    got_c = swap(low_c, "x")
    got_m = after(swap(low_m, "x"), got_c)
    g_last, gg2, low_e, dgu_enc, part, part_low = ffn_back(
        False, enc_last, part_m, got_m, cots[1], gains, gu_enc, ffn_enc, ffn_enc_sib, "enc_ffn_back"
    )
    d_ffn_enc = ffn_weights(n_1, dgu_enc, hid_enc, low_e, "enc_ffn_weights")
    got_e = swap(part_low, "x")
    got_c = after(got_c, *d_ffn_enc)
    d_ffn_enc = both(*d_ffn_enc)
    g_dec, gg4, low_b, dq_dec, mine, other, d_table_dec = attend_local_back(
        4,
        True,
        dec_scalars,
        g,
        dec_mid,
        part_c,
        got_c,
        gains,
        *out_dec,
        q_dec,
        kv_dec,
        kv_dec_got,
        p_dec,
        ctx_dec,
        name="dec_attend_back",
    )
    got_e = after(got_e, dq_dec, d_ffn_dec)
    dec_other = swap(other, "c")
    dec_mine = mine
    g_enc, gg1, low_a, dq_enc, mine, other, d_table_enc = attend_local_back(
        1,
        True,
        enc_scalars,
        g_last,
        enc_mid,
        part,
        got_e,
        gains,
        out_enc,
        out_enc_sib,
        q_enc,
        kv_enc,
        kv_enc_got,
        p_enc,
        ctx_enc,
        name="enc_attend_back",
    )
    dkv_dec, part_d, low = project_back(
        False, dq_dec, dec_mine, dec_other, *w_dec, 0, "dec_project_back"
    )
    got_d = swap(low, "x")
    d_in, d_out, d_in_sib, d_out_sib = attend_weights(
        "attend_weights",
        (n_b, n_b, dq_dec, dkv_dec, ctx_dec, low_b),
        (n_c, memory_low, dq_cross, dkv_cross, ctx_cross, low_x),
    )
    d_out = both(d_out, d_out_sib)
    d_out = jnp.stack([turned_parts(d_out[k], depth) for k in range(2)], 1)
    late = [blocks(d_ffn_enc), blocks(both(d_in, d_in_sib)), pack_out(d_out)]
    late = scatter(jnp.concatenate(late, axis=2))
    got = after(swap(other, "c"), dkv_dec)
    dkv_enc, part, low = project_back(
        False, dq_enc, mine, got, *w_self, 2 * WIDTH, "enc_project_back"
    )
    d_in, d_out, d_in_sib, d_out_sib = attend_weights(
        "enc_attend_weights", (n_a, n_a, dq_enc, dkv_enc, ctx_enc, low_a)
    )
    got = after(swap(low, "x"), d_in, d_out)
    thirds = turned_parts(both(d_out, d_out_sib)[0], depth).reshape(2 * depth, own, 3, D // 3)
    thirds = thirds.transpose(0, 2, 1, 3).reshape(2 * depth, 3 * own, D // 3)
    thirds = jnp.pad(thirds, ((0, 0), (0, group - 3 * own), (0, 0)))
    d_enc = jnp.concatenate([thirds, blocks(both(d_in, d_in_sib))], axis=2)
    d_enc = scatter_y(place, d_enc)
    got_d = after(got_d, d_in)
    grad_dec, gg3 = input_back(3, g_dec, dec_rows, part_d, got_d, gains, "dec_input_back")
    grad_enc, gg0 = input_back(0, g_enc, enc_rows, part, got, gains, "enc_input_back")
    memory_low, dec_final, grad_enc, grad_dec, gg0, gg3 = after(
        (memory_low, dec_final, grad_enc, grad_dec, gg0, gg3), d_enc
    )
    d_enc = scatter_z(place, d_enc)

    wide, inner = 2 * units, 6 * WIDTH
    down = wide + 2 * D // 3
    (sums,) = call(
        functools.partial(sums_kernel, own),
        "column_sums",
        [((64, 128), F32)],
        [late, d_ffn_dec, d_enc],
        1.0,
    )
    out_enc_mine = d_enc[: 3 * own, : D // 3].reshape(3, own, D // 3).transpose(1, 0, 2)
    out_mine = unpack_out_piece(late[:, down + inner :])
    turned_out = jnp.concatenate([rounded(out_enc_mine.reshape(1, own, D)), out_mine])
    turned_out = turn(turned_out, depth).astype(F32)
    columns = [d_ffn_dec[:, :wide], late[:, down : down + inner]]
    columns += [rounded(d_enc[:, D // 3 : D // 3 + 3 * WIDTH]), late[:, :wide]]
    columns = jnp.concatenate(columns, axis=1).reshape(WAYS, own, -1)
    columns = exchange_over_x(place, columns)
    columns_here = columns
    columns = exchange_over_cores(place, columns).astype(F32)
    shard_in, shard_out, shard_hin, shard_hout, row_in, row_out, row_hin, row_hout = call(
        functools.partial(shards_kernel, ff_own),
        "shards",
        [
            ((3, 3, own, D), F32),
            ((3, own, D), F32),
            ((2, 2, own, WAYS * units), F32),
            ((2, ff_own, D), F32),
            ((9, own), F32),
            ((3, own), F32),
            ((4, own), F32),
            ((2, ff_own), F32),
        ],
        [columns, turned_out, late, d_ffn_dec],
        2.0,
    )
    sums = sums + sum(shift_z(sums, k, depth) for k in range(1, depth))
    sums = sums + swap(sums, "y")
    (sums,) = call(hold_kernel, "hold", [(sums.shape, F32)], [sums, (columns_here, ANYWHERE)], 0.3)
    sums = pair_up(sums, swap(sums, "x"), place.x)
    sums = pair_up(sums, swap(sums, "c"), place.c)
    sums = sums.swapaxes(0, 1).reshape(WAYS, -1)
    cuts = [2 * wide, 2 * wide + 9 * WIDTH, 30 * 128, 30 * 128 + 2 * D, 30 * 128 + 5 * D]
    col_hin, col_in, _, col_hout, col_out, _ = jnp.split(sums, cuts, axis=1)
    col_hin = col_hin.reshape(WAYS, 2, 2, 2 * depth, ff_own).transpose(1, 2, 3, 0, 4)
    col_hin = col_hin.reshape(2, 2, WAYS * units)
    col_in = col_in.reshape(WAYS, 9, WIDTH)
    col_in = jnp.stack([col_in[:, k] for k in IN_ORDER]).reshape(3, 3, D)
    col_hout = jnp.sum(col_hout, axis=0).reshape(2, D)
    col_out = jnp.sum(col_out, axis=0).reshape(3, D)

    buckets = position_bias.shape[1]

    def head_table(d_table):
        wide_table = jnp.zeros((2 * SETS, 2 * length + block), F32)
        return lax.dynamic_update_slice_in_dim(wide_table, d_table, block * (1 - place.c), 1)

    grad_enc_bias = head_table(d_table_enc)[:, : 2 * length - 1]
    grad_dec_bias = head_table(d_table_dec)[:, :length][:, ::-1]
    by_set = jnp.stack(
        [
            bucket_grad(enc_buckets, grad_enc_bias, buckets),
            bucket_grad(dec_buckets, grad_dec_bias, buckets),
        ]
    )
    grad_position = lax.dynamic_update_slice_in_dim(
        jnp.zeros_like(position_bias), by_set[:, :, :SETS], q * SETS, 2
    )
    grad_position = lax.dynamic_update_slice_in_dim(
        grad_position, by_set[:, :, SETS:], (q + 1 - 2 * place.c) * SETS, 2
    )
    grad_gains = jnp.concatenate([gg0, gg1, gg2, gg3, gg4, gg5, gg6])
    grad_gains = jnp.where(place.x == 0, grad_gains, 0.0)
    small = jnp.concatenate([grad_gains.reshape(-1, 128), grad_position.reshape(-1, 128)])
    small = sum_everywhere(place, small)
    cut = grad_gains.size // 128
    grad_gains = small[:cut].reshape(grad_gains.shape)
    grad_position = small[cut:].reshape(grad_position.shape)
    shard_gains = lax.dynamic_slice_in_dim(grad_gains, place.index * own, own, 1)

    return (
        give_back(place, memory_low),
        give_back(place, dec_final),
        give_back(place, grad_enc),
        give_back(place, grad_dec),
        shard_in,
        shard_out,
        shard_hin,
        shard_hout,
        shard_gains,
        grad_position,
        row_in.reshape(3, 3, own),
        col_in,
        row_out,
        col_out,
        row_hin.reshape(2, 2, own),
        col_hin,
        row_hout,
        col_hout,
    )


def specs(seq):
    rows = P("dp", seq, None)
    every = ("dp",) + (seq if isinstance(seq, tuple) else (seq,))
    second, third = P(None, every, None), P(None, None, every, None)
    ins = (rows, rows, P("dp"), P("dp"), P(), P(), third, second, third, second)
    ins += (P(None, every), P(), rows, rows)
    outs = (rows, rows, rows, rows, third, second, third, second, P(None, every), P())
    outs += (P(None, None, every), P(), P(None, every), P())
    outs += (P(None, None, every), P(), P(None, every), P())
    return ins, outs


def solution(mesh):
    depth, seq = mesh.shape["dp"], mesh.shape["seq"]

    def wrap(function, over, axes):
        ins, outs = specs(axes)
        return jax.shard_map(function, mesh=over, in_specs=ins, out_specs=outs, check_vma=False)

    def run(*args):
        seqs, length = args[0].shape[0] // depth, args[0].shape[1]
        fits = depth == WAYS and seq == 8 and seqs == 2 and length % 512 == 0
        if fits and args[1].shape == args[0].shape:
            axes = ("y", "x", "c")
            split = Mesh(mesh.devices.reshape(depth, 2, 2, 2), ("dp",) + axes)
            return wrap(functools.partial(grouped, depth), split, axes)(*args)
        return wrap(local, mesh, "seq")(*args)

    return run
```

profile of v0, /device:TPU:0, one launch (start us, length us, event | category | flops | bytes accessed | tf_op | source)
XLA Modules:
  0.0 455.6 jit_solution(475978046009998578)
XLA Ops:
  11.3 3.0 collective-permute-start.2
  15.6 8.9 %collective-permute-done.2 = bf16[2,24,3840]{2,1,0:T(8,128)(2,1)S(1)} collective-permute-done((bf16[2,24,3840]{2,1,0:T(8,128)(2,1)S(1)}, bf16[2,24,3840]{2,1,0:T(8,128)(2,1)S(1)}, u32[]{:S(2)}, u32[]{:S(2)}) %collective-permute-start.2) | collective-permute-done | bytes 368672 | tf_op jit(solution)/shard_map/ppermute | solution.py:705
  31.7 3.6 collective-permute-start.6
  38.4 14.2 %collective-permute-done.6 = bf16[96,896]{1,0:T(8,128)(2,1)S(1)} collective-permute-done((bf16[96,896]{1,0:T(8,128)(2,1)S(1)}, bf16[96,896]{1,0:T(8,128)(2,1)S(1)}, u32[]{:S(2)}, u32[]{:S(2)}) %collective-permute-start.6) | collective-permute-done | bytes 172064 | tf_op jit(solution)/shard_map/ppermute | solution.py:709
  56.4 12.7 %collective-permute-done.8 = bf16[4,96,896]{2,1,0:T(8,128)(2,1)S(1)} collective-permute-done((bf16[4,96,896]{2,1,0:T(8,128)(2,1)S(1)}, bf16[4,96,896]{2,1,0:T(8,128)(2,1)S(1)}, u32[]{:S(2)}, u32[]{:S(2)}) %collective-permute-start.8) | collective-permute-done | bytes 688160 | tf_op jit(solution)/shard_map/ppermute | solution.py:705
  80.5 5.7 %enc_attend.1 = (f32[2,256,192]{2,1,0:T(8,128)S(1)}, bf16[6,256,512]{2,1,0:T(8,128)(2,1)S(1)}, f32[256,768]{1,0:T(8,128)S(1)}, bf16[256,768]{1,0:T(8,128)(2,1)S(1)}) custom-call(s32[2]{0:T(128)S(1)} %pad_add_fusion.refs_0_, bf16[2,256,192]{2,1,0:T(8,128)(2,1)S(1)} %copy-done.61, bf16[2,256,384]{2,1,0:T(8,128)(2,1)} %get-tuple-element.142.refs_2_.refs_9_, ...), custom_call_target="tpu_custom_call" | custom-call | flops 55000000 | bytes 148224 | tf_op jit(solution)/shard_map/enc_attend/pallas_call | solution.py:833
  90.5 10.2 %collective-permute-done.11.refs_2_ = bf16[256,768]{1,0:T(8,128)(2,1)S(1)} collective-permute-done((bf16[256,768]{1,0:T(8,128)(2,1)S(1)}, bf16[256,768]{1,0:T(8,128)(2,1)S(1)}, u32[]{:S(2)}, u32[]{:S(2)}) %collective-permute-start.11) | collective-permute-done | bytes 393248 | tf_op jit(solution)/shard_map/ppermute | solution.py:705
  101.5 18.7 %all-gather.3.cloned.1.call-done.refs_2_.refs_3_.refs_4_.refs_6_ = bf16[768,3072]{1,0:T(8,128)(2,1)} async-done(((bf16[96,3072]{1,0:T(8,128)(2,1)}), bf16[768,3072]{1,0:T(8,128)(2,1)}) %all-gather.3.cloned.1.call-update) | async-done | bytes 4718608 | tf_op jit(solution)/shard_map/all_gather | solution.py:1503
  135.2 5.3 %dec_attend.1 = (f32[2,256,192]{2,1,0:T(8,128)S(1)}, bf16[6,256,512]{2,1,0:T(8,128)(2,1)S(1)}, f32[256,768]{1,0:T(8,128)S(1)}, bf16[256,768]{1,0:T(8,128)(2,1)S(1)}) custom-call(s32[2]{0:T(128)S(1)} %pad_add_fusion.1.refs_0_, bf16[2,256,192]{2,1,0:T(8,128)(2,1)S(1)} %get-tuple-element.146.refs_1_.refs_8_, ...), custom_call_target="tpu_custom_call" | custom-call | flops 55000000 | bytes 166656 | tf_op jit(solution)/shard_map/dec_attend/pallas_call | solution.py:833
  144.6 3.7 enc_ffn.1
  148.4 6.1 %collective-permute-done.15.refs_2_ = bf16[256,768]{1,0:T(8,128)(2,1)S(1)} collective-permute-done((bf16[256,768]{1,0:T(8,128)(2,1)S(1)}, bf16[256,768]{1,0:T(8,128)(2,1)S(1)}, u32[]{:S(2)}, u32[]{:S(2)}) %collective-permute-start.15) | collective-permute-done | bytes 393248 | tf_op jit(solution)/shard_map/ppermute | solution.py:705
  158.1 4.5 collective-permute-done.14.refs_2_
  167.8 3.8 cross_attend.1
  177.8 9.8 %collective-permute-done.17.refs_2_ = bf16[256,768]{1,0:T(8,128)(2,1)S(1)} collective-permute-done((bf16[256,768]{1,0:T(8,128)(2,1)}, bf16[256,768]{1,0:T(8,128)(2,1)S(1)}, u32[]{:S(2)}, u32[]{:S(2)}) %collective-permute-start.17) | collective-permute-done | bytes 393248 | tf_op jit(solution)/shard_map/ppermute | solution.py:705
  191.6 11.9 %dec_ffn.1 = (f32[256,768]{1,0:T(8,128)S(1)}, bf16[256,768]{1,0:T(8,128)(2,1)S(1)}, f32[2,256,1024]{2,1,0:T(8,128)S(1)}, bf16[2,256,512]{2,1,0:T(8,128)(2,1)S(1)...) custom-call(f32[256,768]{1,0:T(8,128)S(1)} %copy-done.19, f32[256,768]{1,0:T(8,128)S(1)} %copy-done.77, ...), custom_call_target="tpu_custom_call" | custom-call | flops 30000000 | bytes 365216 | tf_op jit(solution)/shard_map/dec_ffn/pallas_call | solution.py:833
  205.3 8.8 %collective-permute-done.19.refs_2_ = bf16[256,768]{1,0:T(8,128)(2,1)S(1)} collective-permute-done((bf16[256,768]{1,0:T(8,128)(2,1)S(1)}, bf16[256,768]{1,0:T(8,128)(2,1)S(1)}, u32[]{:S(2)}, u32[]{:S(2)}) %collective-permute-start.19) | collective-permute-done | bytes 393248 | tf_op jit(solution)/shard_map/ppermute | solution.py:705
  224.9 5.0 %collective-permute-done.20.refs_4_ = bf16[256,768]{1,0:T(8,128)(2,1)S(1)} collective-permute-done((bf16[256,768]{1,0:T(8,128)(2,1)S(1)}, bf16[256,768]{1,0:T(8,128)(2,1)S(1)}, u32[]{:S(2)}, u32[]{:S(2)}) %collective-permute-start.20) | collective-permute-done | bytes 393248 | tf_op jit(solution)/shard_map/ppermute | solution.py:705
  229.9 6.2 %cross_attend_back.1 = (f32[256,768]{1,0:T(8,128)S(1)}, f32[1,768]{1,0:T(1,128)S(1)}, bf16[256,768]{1,0:T(8,128)(2,1)S(1)}, bf16[2,256,192]{2,1,0:T(8,128)(2,1)S...) custom-call(s32[2]{0:T(128)S(1)} %pad_add_fusion.refs_0_, f32[256,768]{1,0:T(8,128)S(1)} %get-tuple-element.169.refs_1_, ...), custom_call_target="tpu_custom_call" | custom-call | flops 60000000 | bytes 295680 | tf_op jit(solution)/shard_map/cross_attend_back/pallas_call | solution.py:833
  250.4 9.9 %collective-permute-done.23.refs_2_ = bf16[256,768]{1,0:T(8,128)(2,1)S(1)} collective-permute-done((bf16[256,768]{1,0:T(8,128)(2,1)S(1)}, bf16[256,768]{1,0:T(8,128)(2,1)S(1)}, u32[]{:S(2)}, u32[]{:S(2)}) %collective-permute-start.23) | collective-permute-done | bytes 393248 | tf_op jit(solution)/shard_map/ppermute | solution.py:705
  260.3 7.7 %collective-permute-done.24.refs_4_ = bf16[256,768]{1,0:T(8,128)(2,1)S(1)} collective-permute-done((bf16[256,768]{1,0:T(8,128)(2,1)S(1)}, bf16[256,768]{1,0:T(8,128)(2,1)S(1)}, u32[]{:S(2)}, u32[]{:S(2)}) %collective-permute-start.24) | collective-permute-done | bytes 393248 | tf_op jit(solution)/shard_map/ppermute | solution.py:705
  268.0 4.7 %enc_ffn_back.1 = (f32[256,768]{1,0:T(8,128)S(1)}, f32[1,768]{1,0:T(1,128)S(1)}, bf16[256,768]{1,0:T(8,128)(2,1)S(1)}, bf16[2,256,1024]{2,1,0:T(8,128)(2,1)S(1)}...) custom-call(f32[256,768]{1,0:T(8,128)S(1)} %copy-done.69, f32[256,768]{1,0:T(8,128)S(1)} %get-tuple-element.184.refs_1_, ...), custom_call_target="tpu_custom_call" | custom-call | flops 40000000 | bytes 541440 | tf_op jit(solution)/shard_map/enc_ffn_back/pallas_call | solution.py:833
  275.6 9.7 %dec_attend_back.1 = (f32[256,768]{1,0:T(8,128)S(1)}, f32[1,768]{1,0:T(1,128)S(1)}, bf16[256,768]{1,0:T(8,128)(2,1)S(1)}, bf16[2,256,192]{2,1,0:T(8,128)(2,1)S(1...) custom-call(s32[2]{0:T(128)S(1)} %pad_add_fusion.1.refs_0_, ...), custom_call_target="tpu_custom_call" | custom-call | flops 90000000 | bytes 296448 | tf_op jit(solution)/shard_map/dec_attend_back/pallas_call | solution.py:833
  288.0 3.0 dec_project_back.1
  294.4 7.3 %collective-permute-done.39 = bf16[2,192,768]{2,1,0:T(8,128)(2,1)S(1)} collective-permute-done((bf16[2,192,768]{2,1,0:T(8,128)(2,1)S(1)}, bf16[2,192,768]{2,1,0:T(8,128)(2,1)S(1)}, u32[]{:S(2)}, u32[]{:S(2)}) %collective-permute-start.39) | collective-permute-done | bytes 589856 | tf_op jit(solution)/shard_map/ppermute | solution.py:705
  307.6 9.6 %collective-permute-done.25.refs_4_ = bf16[256,768]{1,0:T(8,128)(2,1)S(1)} collective-permute-done((bf16[256,768]{1,0:T(8,128)(2,1)}, bf16[256,768]{1,0:T(8,128)(2,1)S(1)}, u32[]{:S(2)}, u32[]{:S(2)}) %collective-permute-start.25) | collective-permute-done | bytes 393248 | tf_op jit(solution)/shard_map/ppermute | solution.py:705
  327.7 9.7 %enc_attend_back.1 = (f32[256,768]{1,0:T(8,128)S(1)}, f32[1,768]{1,0:T(1,128)S(1)}, bf16[256,768]{1,0:T(8,128)(2,1)S(1)}, bf16[2,256,192]{2,1,0:T(8,128)(2,1)S(1...) custom-call(s32[2]{0:T(128)S(1)} %pad_add_fusion.refs_0_, ...), custom_call_target="tpu_custom_call" | custom-call | flops 90000000 | bytes 278016 | tf_op jit(solution)/shard_map/enc_attend_back/pallas_call | solution.py:833
  356.4 6.9 %collective-permute-done.29.refs_3_ = bf16[256,768]{1,0:T(8,128)(2,1)} collective-permute-done((bf16[256,768]{1,0:T(8,128)(2,1)}, bf16[256,768]{1,0:T(8,128)(2,1)}, u32[]{:S(2)}, u32[]{:S(2)}) %collective-permute-start.29) | collective-permute-done | bytes 393248 | tf_op jit(solution)/shard_map/ppermute | solution.py:705
  365.7 4.7 %collective-permute-done.28.refs_3_ = bf16[256,768]{1,0:T(8,128)(2,1)S(1)} collective-permute-done((bf16[256,768]{1,0:T(8,128)(2,1)}, bf16[256,768]{1,0:T(8,128)(2,1)S(1)}, u32[]{:S(2)}, u32[]{:S(2)}) %collective-permute-start.28) | collective-permute-done | bytes 393248 | tf_op jit(solution)/shard_map/ppermute | solution.py:705
  386.9 4.4 collective-permute-start.49
  400.3 4.1 collective-permute-done.34
  430.5 3.1 collective-permute-done.55
  445.4 2.8 shards.1
  (581 shorter events, 209.9 us)
Async XLA Ops:
  7.2 112.9 %all-gather.3.cloned.1.call-start = ((), (), s32[]{:S(2)}) async-start(), calls=%async_computation.2 | async-start | bytes 5308416 | tf_op jit(solution)/shard_map/all_gather | solution.py:1503
  11.3 13.3 %collective-permute-start.2 = (bf16[2,24,3840]{2,1,0:T(8,128)(2,1)S(1)}, bf16[2,24,3840]{2,1,0:T(8,128)(2,1)S(1)}, u32[]{:S(2)}, u32[]{:S(2)}) collective-permute-start(bf16[2,24,3840]{2,1,0:T(8,128)(2,1)S(1)} %dynamic-slice_bitcast_fusion.1), channel_id=1, source_target_pairs={{0,2},{2,0},{1,3},{3,1},{4,6},{6,4},{5,7},{7,5},{8,10},{10,8},{9,1... | collective-permute-start | bytes 1105928 | tf_op jit(solution)/shard_map/ppermute | solution.py:705
  14.3 10.5 %collective-permute-start.4 = (bf16[3,24,768]{2,1,0:T(8,128)(2,1)S(1)}, bf16[3,24,768]{2,1,0:T(8,128)(2,1)S(1)}, u32[]{:S(2)}, u32[]{:S(2)}) collective-permute-start(bf16[3,24,768]{2,1,0:T(8,128)(2,1)S(1)} %copy-done.122), channel_id=1, source_target_pairs={{0,0},{1,8},{2,16},{3,24},{4,4},{5,12},{6,20},{7,28},{8,1},{9,9},{... | collective-permute-start | bytes 331784 | tf_op jit(solution)/shard_map/ppermute | solution.py:789
  28.2 147.7 %all-gather.5.cloned.1.call-start = ((), (), s32[]{:S(2)}) async-start(), calls=%async_computation.3 | async-start | bytes 2654208 | tf_op jit(solution)/shard_map/all_gather | solution.py:1503
  28.5 9.9 %collective-permute-start.5 = (bf16[96,896]{1,0:T(8,128)(2,1)S(1)}, bf16[96,896]{1,0:T(8,128)(2,1)S(1)}, u32[]{:S(2)}, u32[]{:S(2)}) collective-permute-start(bf16[96,896]{1,0:T(8,128)(2,1)S(1)} %fusion.25), channel_id=1, source_target_pairs={{0,8},{8,16},{16,24},{24,0},{1,9},{9,17},{17,25},{25,1},{2,10},{10... | collective-permute-start | bytes 516104 | tf_op jit(solution)/shard_map/ppermute | solution.py:709
  30.2 24.8 %collective-permute-start = (bf16[4,64,768]{2,1,0:T(8,128)(2,1)S(1)}, bf16[4,64,768]{2,1,0:T(8,128)(2,1)S(1)}, u32[]{:S(2)}, u32[]{:S(2)}) collective-permute-start(bf16[4,64,768]{2,1,0:T(8,128)(2,1)S(1)} %pad_maximum_fusion.8), channel_id=1, source_target_pairs={{0,4},{4,0},{1,5},{5,1},{2,6},{6,2},{3,7},{7,3},{8,12},{12,8},{9,1... | collective-permute-start | bytes 1179656 | tf_op jit(solution)/shard_map/ppermute | solution.py:705
  31.7 20.9 %collective-permute-start.6 = (bf16[96,896]{1,0:T(8,128)(2,1)S(1)}, bf16[96,896]{1,0:T(8,128)(2,1)S(1)}, u32[]{:S(2)}, u32[]{:S(2)}) collective-permute-start(bf16[96,896]{1,0:T(8,128)(2,1)S(1)} %fusion.25), channel_id=1, source_target_pairs={{0,16},{8,24},{16,0},{24,8},{1,17},{9,25},{17,1},{25,9},{2,18},{10... | collective-permute-start | bytes 516104 | tf_op jit(solution)/shard_map/ppermute | solution.py:709
  35.3 17.4 %collective-permute-start.7 = (bf16[96,896]{1,0:T(8,128)(2,1)S(1)}, bf16[96,896]{1,0:T(8,128)(2,1)S(1)}, u32[]{:S(2)}, u32[]{:S(2)}) collective-permute-start(bf16[96,896]{1,0:T(8,128)(2,1)S(1)} %fusion.25), channel_id=1, source_target_pairs={{0,24},{8,0},{16,8},{24,16},{1,25},{9,1},{17,9},{25,17},{2,26},{10... | collective-permute-start | bytes 516104 | tf_op jit(solution)/shard_map/ppermute | solution.py:709
  52.7 16.4 %collective-permute-start.8 = (bf16[4,96,896]{2,1,0:T(8,128)(2,1)S(1)}, bf16[4,96,896]{2,1,0:T(8,128)(2,1)S(1)}, u32[]{:S(2)}, u32[]{:S(2)}) collective-permute-start(bf16[4,96,896]{2,1,0:T(8,128)(2,1)S(1)} %bitcast_dynamic-update-slice_fusion), channel_id=1, source_target_pairs={{0,4},{4,0},{1,5},{5,1},{2,6},{6,2},{3,7},{7,3},{8,12},{12,8},{9,1... | collective-permute-start | bytes 2064392 | tf_op jit(solution)/shard_map/ppermute | solution.py:705
  55.1 18.2 %collective-permute-start.1 = (bf16[2,4,64,768]{3,2,1,0:T(8,128)(2,1)S(1)}, bf16[2,4,64,768]{3,2,1,0:T(8,128)(2,1)S(1)}, u32[]{:S(2)}, u32[]{:S(2)}) collective-permute-start(bf16[2,4,64,768]{3,2,1,0:T(8,128)(2,1)S(1)} %pad_maximum_fusion.2), channel_id=1, source_target_pairs={{0,2},{2,0},{1,3},{3,1},{4,6},{6,4},{5,7},{7,5},{8,10},{10,8},{9,1... | collective-permute-start | bytes 2359304 | tf_op jit(solution)/shard_map/ppermute | solution.py:705
  89.2 11.5 %collective-permute-start.11 = (bf16[256,768]{1,0:T(8,128)(2,1)S(1)}, bf16[256,768]{1,0:T(8,128)(2,1)S(1)}, u32[]{:S(2)}, u32[]{:S(2)}) collective-permute-start(bf16[256,768]{1,0:T(8,128)(2,1)S(1)} %get-tuple-element.144), channel_id=1, source_target_pairs={{0,2},{2,0},{1,3},{3,1},{4,6},{6,4},{5,7},{7,5},{8,10},{10,8},{9,1... | collective-permute-start | bytes 1179656 | tf_op jit(solution)/shard_map/ppermute | solution.py:705
  121.9 196.0 %reduce-scatter.3.cloned.1.call-start = ((), (), s32[]{:S(2)}) async-start(), calls=%async_computation.4 | async-start | bytes 2654208 | tf_op jit(solution)/shard_map/reduce_scatter | solution.py:1600
  142.4 12.0 %collective-permute-start.15 = (bf16[256,768]{1,0:T(8,128)(2,1)S(1)}, bf16[256,768]{1,0:T(8,128)(2,1)S(1)}, u32[]{:S(2)}, u32[]{:S(2)}) collective-permute-start(bf16[256,768]{1,0:T(8,128)(2,1)S(1)} %get-tuple-element.148), channel_id=1, source_target_pairs={{0,2},{2,0},{1,3},{3,1},{4,6},{6,4},{5,7},{7,5},{8,10},{10,8},{9,1... | collective-permute-start | bytes 1179656 | tf_op jit(solution)/shard_map/ppermute | solution.py:705
  148.3 14.3 %collective-permute-start.14 = (bf16[256,768]{1,0:T(8,128)(2,1)S(1)}, bf16[256,768]{1,0:T(8,128)(2,1)S(1)}, u32[]{:S(2)}, u32[]{:S(2)}) collective-permute-start(bf16[256,768]{1,0:T(8,128)(2,1)S(1)} %get-tuple-element.152), channel_id=1, source_target_pairs={{0,2},{2,0},{1,3},{3,1},{4,6},{6,4},{5,7},{7,5},{8,10},{10,8},{9,1... | collective-permute-start | bytes 1179656 | tf_op jit(solution)/shard_map/ppermute | solution.py:705
  175.9 11.7 %collective-permute-start.18 = (bf16[768,1536]{1,0:T(8,128)(2,1)}, bf16[768,1536]{1,0:T(8,128)(2,1)S(1)}, u32[]{:S(2)}, u32[]{:S(2)}) collective-permute-start(bf16[768,1536]{1,0:T(8,128)(2,1)} %all-gather.5.cloned.1.call-done.refs_4_.refs_6_), channel_id=1, source_target_pairs={{0,1},{1,0},{2,3},{3,2},{4,5},{5,4},{6,7},{7,6},{8,9},{9,8},{10,11... | collective-permute-start | bytes 7077896 | tf_op jit(solution)/shard_map/ppermute | solution.py:705
  176.0 11.6 %collective-permute-start.17 = (bf16[256,768]{1,0:T(8,128)(2,1)}, bf16[256,768]{1,0:T(8,128)(2,1)S(1)}, u32[]{:S(2)}, u32[]{:S(2)}) collective-permute-start(bf16[256,768]{1,0:T(8,128)(2,1)} %copy-done.105), channel_id=1, source_target_pairs={{0,2},{2,0},{1,3},{3,1},{4,6},{6,4},{5,7},{7,5},{8,10},{10,8},{9,1... | collective-permute-start | bytes 1179656 | tf_op jit(solution)/shard_map/ppermute | solution.py:705
  203.5 10.7 %collective-permute-start.19 = (bf16[256,768]{1,0:T(8,128)(2,1)S(1)}, bf16[256,768]{1,0:T(8,128)(2,1)S(1)}, u32[]{:S(2)}, u32[]{:S(2)}) collective-permute-start(bf16[256,768]{1,0:T(8,128)(2,1)S(1)} %get-tuple-element.165), channel_id=1, source_target_pairs={{0,2},{2,0},{1,3},{3,1},{4,6},{6,4},{5,7},{7,5},{8,10},{10,8},{9,1... | collective-permute-start | bytes 1179656 | tf_op jit(solution)/shard_map/ppermute | solution.py:705
  218.3 11.5 %collective-permute-start.20 = (bf16[256,768]{1,0:T(8,128)(2,1)S(1)}, bf16[256,768]{1,0:T(8,128)(2,1)S(1)}, u32[]{:S(2)}, u32[]{:S(2)}) collective-permute-start(bf16[256,768]{1,0:T(8,128)(2,1)S(1)} %get-tuple-element.171), channel_id=1, source_target_pairs={{0,2},{2,0},{1,3},{3,1},{4,6},{6,4},{5,7},{7,5},{8,10},{10,8},{9,1... | collective-permute-start | bytes 1179656 | tf_op jit(solution)/shard_map/ppermute | solution.py:705
  239.4 180.6 %reduce-scatter.5.cloned.1.call-start = ((), (), s32[]{:S(2)}) async-start(), calls=%async_computation.5 | async-start | bytes 5308416 | tf_op jit(solution)/shard_map/reduce_scatter | solution.py:1600
  248.2 12.0 %collective-permute-start.23 = (bf16[256,768]{1,0:T(8,128)(2,1)S(1)}, bf16[256,768]{1,0:T(8,128)(2,1)S(1)}, u32[]{:S(2)}, u32[]{:S(2)}) collective-permute-start(bf16[256,768]{1,0:T(8,128)(2,1)S(1)} %get-tuple-element.185), channel_id=1, source_target_pairs={{0,2},{2,0},{1,3},{3,1},{4,6},{6,4},{5,7},{7,5},{8,10},{10,8},{9,1... | collective-permute-start | bytes 1179656 | tf_op jit(solution)/shard_map/ppermute | solution.py:705
  250.1 17.9 %collective-permute-start.24 = (bf16[256,768]{1,0:T(8,128)(2,1)S(1)}, bf16[256,768]{1,0:T(8,128)(2,1)S(1)}, u32[]{:S(2)}, u32[]{:S(2)}) collective-permute-start(bf16[256,768]{1,0:T(8,128)(2,1)S(1)} %get-tuple-element.186), channel_id=1, source_target_pairs={{0,2},{2,0},{1,3},{3,1},{4,6},{6,4},{5,7},{7,5},{8,10},{10,8},{9,1... | collective-permute-start | bytes 1179656 | tf_op jit(solution)/shard_map/ppermute | solution.py:705
  293.7 8.4 %collective-permute-start.38 = (bf16[768,1152]{1,0:T(8,128)(2,1)S(1)}, bf16[768,1152]{1,0:T(8,128)(2,1)S(1)}, u32[]{:S(2)}, u32[]{:S(2)}) collective-permute-start(bf16[768,1152]{1,0:T(8,128)(2,1)S(1)} %get-tuple-element.244), channel_id=1, source_target_pairs={{0,1},{1,0},{2,3},{3,2},{4,5},{5,4},{6,7},{7,6},{8,9},{9,8},{10,11... | collective-permute-start | bytes 5308424 | tf_op jit(solution)/shard_map/ppermute | solution.py:705
  293.9 8.7 %collective-permute-start.37 = (bf16[768,1536]{1,0:T(8,128)(2,1)S(1)}, bf16[768,1536]{1,0:T(8,128)(2,1)S(1)}, u32[]{:S(2)}, u32[]{:S(2)}) collective-permute-start(bf16[768,1536]{1,0:T(8,128)(2,1)S(1)} %get-tuple-element.199), channel_id=1, source_target_pairs={{0,1},{1,0},{2,3},{3,2},{4,5},{5,4},{6,7},{7,6},{8,9},{9,8},{10,11... | collective-permute-start | bytes 7077896 | tf_op jit(solution)/shard_map/ppermute | solution.py:705
  305.8 11.4 %collective-permute-start.25 = (bf16[256,768]{1,0:T(8,128)(2,1)}, bf16[256,768]{1,0:T(8,128)(2,1)S(1)}, u32[]{:S(2)}, u32[]{:S(2)}) collective-permute-start(bf16[256,768]{1,0:T(8,128)(2,1)} %copy-done.104), channel_id=1, source_target_pairs={{0,2},{2,0},{1,3},{3,1},{4,6},{6,4},{5,7},{7,5},{8,10},{10,8},{9,1... | collective-permute-start | bytes 1179656 | tf_op jit(solution)/shard_map/ppermute | solution.py:705
  349.4 25.1 %collective-permute-start.32 = (bf16[4,96,896]{2,1,0:T(8,128)(2,1)}, bf16[4,96,896]{2,1,0:T(8,128)(2,1)}, u32[]{:S(2)}, u32[]{:S(2)}) collective-permute-start(bf16[4,96,896]{2,1,0:T(8,128)(2,1)} %fusion.1), channel_id=1, source_target_pairs={{0,4},{4,0},{1,5},{5,1},{2,6},{6,2},{3,7},{7,3},{8,12},{12,8},{9,1... | collective-permute-start | bytes 2064392 | tf_op jit(solution)/shard_map/ppermute | solution.py:705
  351.0 12.3 %collective-permute-start.29 = (bf16[256,768]{1,0:T(8,128)(2,1)}, bf16[256,768]{1,0:T(8,128)(2,1)}, u32[]{:S(2)}, u32[]{:S(2)}) collective-permute-start(bf16[256,768]{1,0:T(8,128)(2,1)} %get-tuple-element.227), channel_id=1, source_target_pairs={{0,2},{2,0},{1,3},{3,1},{4,6},{6,4},{5,7},{7,5},{8,10},{10,8},{9,1... | collective-permute-start | bytes 1179656 | tf_op jit(solution)/shard_map/ppermute | solution.py:705
  352.7 17.8 %collective-permute-start.28 = (bf16[256,768]{1,0:T(8,128)(2,1)}, bf16[256,768]{1,0:T(8,128)(2,1)S(1)}, u32[]{:S(2)}, u32[]{:S(2)}) collective-permute-start(bf16[256,768]{1,0:T(8,128)(2,1)} %get-tuple-element.217), channel_id=1, source_target_pairs={{0,2},{2,0},{1,3},{3,1},{4,6},{6,4},{5,7},{7,5},{8,10},{10,8},{9,1... | collective-permute-start | bytes 1179656 | tf_op jit(solution)/shard_map/ppermute | solution.py:705
  377.8 38.1 %collective-permute-start.40 = (bf16[96,896]{1,0:T(8,128)(2,1)}, bf16[96,896]{1,0:T(8,128)(2,1)S(1)}, u32[]{:S(2)}, u32[]{:S(2)}) collective-permute-start(bf16[96,896]{1,0:T(8,128)(2,1)} %get-tuple-element.328), channel_id=1, source_target_pairs={{0,8},{8,16},{16,24},{24,0},{1,9},{9,17},{17,25},{25,1},{2,10},{10... | collective-permute-start | bytes 516104 | tf_op jit(solution)/shard_map/ppermute | solution.py:709
  377.8 38.1 %collective-permute-start.41 = (bf16[96,896]{1,0:T(8,128)(2,1)}, bf16[96,896]{1,0:T(8,128)(2,1)}, u32[]{:S(2)}, u32[]{:S(2)}) collective-permute-start(bf16[96,896]{1,0:T(8,128)(2,1)} %get-tuple-element.330), channel_id=1, source_target_pairs={{0,16},{8,24},{16,0},{24,8},{1,17},{9,25},{17,1},{25,9},{2,18},{10... | collective-permute-start | bytes 516104 | tf_op jit(solution)/shard_map/ppermute | solution.py:709
  393.7 22.1 %collective-permute-start.42 = (bf16[96,896]{1,0:T(8,128)(2,1)}, bf16[96,896]{1,0:T(8,128)(2,1)}, u32[]{:S(2)}, u32[]{:S(2)}) collective-permute-start(bf16[96,896]{1,0:T(8,128)(2,1)} %get-tuple-element.329), channel_id=1, source_target_pairs={{0,24},{8,0},{16,8},{24,16},{1,25},{9,1},{17,9},{25,17},{2,26},{10... | collective-permute-start | bytes 516104 | tf_op jit(solution)/shard_map/ppermute | solution.py:709
  397.6 19.6 %collective-permute-start.36 = (f32[64,768]{1,0:T(8,128)S(1)}, f32[64,768]{1,0:T(8,128)}, u32[]{:S(2)}, u32[]{:S(2)}) collective-permute-start(f32[64,768]{1,0:T(8,128)S(1)} %dynamic-slice_bitcast_fusion.2), channel_id=1, source_target_pairs={{0,4},{4,0},{1,5},{5,1},{2,6},{6,2},{3,7},{7,3},{8,12},{12,8},{9,1... | collective-permute-start | bytes 589832 | tf_op jit(solution)/shard_map/ppermute | solution.py:705
  429.9 8.5 %collective-permute-start.45 = (bf16[3,24,768]{2,1,0:T(8,128)(2,1)S(1)}, bf16[3,24,768]{2,1,0:T(8,128)(2,1)S(1)}, u32[]{:S(2)}, u32[]{:S(2)}) collective-permute-start(bf16[3,24,768]{2,1,0:T(8,128)(2,1)S(1)} %pad_maximum_fusion.13), channel_id=1, source_target_pairs={{0,0},{1,8},{2,16},{3,24},{4,4},{5,12},{6,20},{7,28},{8,1},{9,9},{... | collective-permute-start | bytes 331784 | tf_op jit(solution)/shard_map/ppermute | solution.py:789
  (161 other events, 1039.8 us)
Sparse Core Ops, SparseCore 0:
  28.3 91.7 all-gather.2
  122.3 50.8 all-gather.4
  239.5 67.8 reduce-scatter.2
  310.9 106.8 reduce-scatter.4
where the time goes:
time: 461 us; the launch traced here: 456 us
  waiting for transfers between devices  187 us (41%)
  Pallas kernels  88.6 us (19%)
  local copies, waits for them, and re-layouts  77.7 us (17%)
  starting transfers between devices  61 us (13%)
  other arithmetic  23.7 us (5%)
  between operations  16.2 us (4%)
    ppermute x44, waiting for transfers between devices, swap(): return lax.ppermute(values, axis, [(0, 1), (1, 0)])  150 us
    pallas_call x26, Pallas kernels, call(): pl.pallas_call(bring_in, grid=(1,) if windows else (), out_shape=shapes,...  88.6 us
    unnamed x268, local copies, waits for them, and re-layouts  52.4 us
    ppermute x44, starting transfers between devices, swap(): return lax.ppermute(values, axis, [(0, 1), (1, 0)])  40 us
    ppermute x12, starting transfers between devices, shift_z(): lax.ppermute(values, 'dp', [(i, (i + hops) % count) for i in range(count)])  19.2 us
    all_gather x2, waiting for transfers between devices, gather(): return lax.all_gather(piece, ('dp', 'y'), axis=0, tiled=True)  18.7 us
    ppermute x12, waiting for transfers between devices, shift_z(): lax.ppermute(values, 'dp', [(i, (i + hops) % count) for i in range(count)])  18.2 us
  transfers between devices with their start and end apart: 62, of which 38 were waited for; matrix products, arithmetic and copies ran while one was open for 10% of the time, Pallas kernels for 14%

commit v1 on v0

--- a/solution.py
+++ b/solution.py
@@ -1332,29 +1332,29 @@
     return sums[:1]
 
 
-def shards_kernel(ff_own, columns_ref, turned_ref, late_ref, dec_ref, *outs):
+def shards_kernel(ff_own, columns_ref, early_ref, turned_ref, late_ref, dec_ref, *outs):
     in_ref, out_ref, hin_ref, hout_ref, row_in_ref, row_out_ref, row_hin_ref, row_hout_ref = outs
     third = D // 3
     width = dec_ref.shape[1]
     wide = width - 2 * third
     units = wide // 2
     for k, at in enumerate(IN_ORDER):
-        at = wide + at * WIDTH
+        ref, at = (columns_ref, at * WIDTH) if at < 6 else (early_ref, wide + (at - 6) * WIDTH)
         for q in range(WAYS):
-            piece = columns_ref[q, :, at : at + WIDTH]
+            piece = ref[q, :, at : at + WIDTH]
             in_ref[k // 3, k % 3, :, q * WIDTH : (q + 1) * WIDTH] = piece
         row_in_ref[k : k + 1, :] = half_mean_rows(in_ref[k // 3, k % 3])
     out_ref[...] = turned_ref[...]
     for k in range(3):
         row_out_ref[k : k + 1, :] = half_mean_rows(turned_ref[k])
     for layer in range(2):
-        begin = wide + 9 * WIDTH if layer == 0 else 0
+        ref, begin = (columns_ref, 6 * WIDTH) if layer == 0 else (early_ref, 0)
         for j in range(2):
             for k in range(units // ff_own):
                 first = begin + j * units + k * ff_own
                 for q in range(WAYS):
                     at = (WAYS * k + q) * ff_own
-                    piece = columns_ref[q, :, first : first + ff_own]
+                    piece = ref[q, :, first : first + ff_own]
                     hin_ref[layer, j, :, at : at + ff_own] = piece
             row_hin_ref[2 * layer + j : 2 * layer + j + 1, :] = half_mean_rows(hin_ref[layer, j])
     for layer, ref in enumerate((late_ref, dec_ref)):
@@ -1479,10 +1479,11 @@
     hidden_pieces = hidden_pieces.transpose(4, 0, 2, 1, 3, 5).reshape(WAYS, 2, own, 2 * units)
     blocks_in = [keys[:, 0], values[:, 0], queries[:, 0], gain_piece]
     blocks_in += [keys[:, 1], values[:, 1], keys[:, 2], values[:, 2], queries[:, 1], queries[:, 2]]
-    blocks_in += [hidden_pieces[:, 0], hidden_pieces[:, 1]]
+    blocks_in += [hidden_pieces[:, 0]]
     everything = exchange_columns(place, jnp.concatenate(blocks_in, axis=2)).reshape(group, -1)
-    cuts = [3 * WIDTH + 64, 9 * WIDTH + 64, 9 * WIDTH + 64 + 2 * units]
-    enc_piece, rest, ffn_enc, ffn_dec = jnp.split(everything, cuts, axis=1)
+    cuts = [3 * WIDTH + 64, 9 * WIDTH + 64]
+    enc_piece, rest, ffn_enc = jnp.split(everything, cuts, axis=1)
+    ffn_dec = exchange_columns(place, after(hidden_pieces[:, 1], ffn_enc)).reshape(group, -1)
     third = turned[0].reshape(own, 3, D // 3).transpose(1, 0, 2).reshape(3 * own, D // 3)
     third = jnp.pad(third, ((0, group - 3 * own), (0, 0)))
     enc_piece = jnp.concatenate([enc_piece, third], axis=1)
@@ -1541,17 +1542,12 @@
     ffn_dec = gather(after(ffn_dec, low_enc))
     got_enc = swap(low_enc, "x")
     first = after(first, got_enc)
-    first_sib = swap(first, "c")
-    rest, rest_sib = first[:, : ffn_enc.shape[1]], first_sib[:, : ffn_enc.shape[1]]
-
+    rest, ffn_enc = first[:, : ffn_enc.shape[1]], first[:, ffn_enc.shape[1] :]
+    rest_sib, ffn_enc_sib = swap(rest, "c"), swap(ffn_enc, "c")
     out_rest = unpack_out(rest[:, 6 * WIDTH :].reshape(2 * depth, group, -1), depth)
     out_rest_sib = unpack_out(rest_sib[:, 6 * WIDTH :].reshape(2 * depth, group, -1), depth)
-    w_dec = [column_block(w, k) for w in (first, first_sib) for k in (0, 2)]
-    w_cross = [column_block(w, k) for w in (first, first_sib) for k in (1, 2)]
-    ffn_width = ffn_enc.shape[1]
-    ffn_enc, ffn_enc_sib = [
-        (w, pl.BlockSpec((D, ffn_width), lambda _: (0, 1))) for w in (first, first_sib)
-    ]
+    w_dec = [column_block(w, k) for w in (rest, rest_sib) for k in (0, 2)]
+    w_cross = [column_block(w, k) for w in (rest, rest_sib) for k in (1, 2)]
     out_dec, out_cross = [[(w, pl.BlockSpec((None, WIDTH, D), f)) for w in (out_rest, out_rest_sib)]
         for f in (lambda _: (0, 0, 0), lambda _: (1, 0, 0))]
 
@@ -1654,7 +1650,7 @@
         ctx_dec,
         name="dec_attend_back",
     )
-    got_e = after(got_e, dq_dec, d_ffn_dec)
+    got_e = after(got_e, dq_dec)
     dec_other = swap(other, "c")
     dec_mine = mine
     g_enc, gg1, low_a, dq_enc, mine, other, d_table_enc = attend_local_back(
@@ -1686,7 +1682,8 @@
     )
     d_out = both(d_out, d_out_sib)
     d_out = jnp.stack([turned_parts(d_out[k], depth) for k in range(2)], 1)
-    late = [blocks(d_ffn_enc), blocks(both(d_in, d_in_sib)), pack_out(d_out)]
+    d_in = d_in.astype(F32) + after(swap(d_in_sib, "c"), d_ffn_dec).astype(F32)
+    late = [blocks(d_ffn_enc), blocks(rounded(d_in)), pack_out(d_out)]
     late = scatter(jnp.concatenate(late, axis=2))
     got = after(swap(other, "c"), dkv_dec)
     dkv_enc, part, low = project_back(
@@ -1710,6 +1707,10 @@
     d_enc = scatter_z(place, d_enc)
 
     wide, inner = 2 * units, 6 * WIDTH
+    early = [d_ffn_dec[:, :wide], rounded(d_enc[:, D // 3 : D // 3 + 3 * WIDTH])]
+    early = jnp.concatenate(early, axis=1).reshape(WAYS, own, -1)
+    early = exchange_columns(place, early).astype(F32)
+    late = after(late, early)
     down = wide + 2 * D // 3
     (sums,) = call(
         functools.partial(sums_kernel, own),
@@ -1722,8 +1723,7 @@
     out_mine = unpack_out_piece(late[:, down + inner :])
     turned_out = jnp.concatenate([rounded(out_enc_mine.reshape(1, own, D)), out_mine])
     turned_out = turn(turned_out, depth).astype(F32)
-    columns = [d_ffn_dec[:, :wide], late[:, down : down + inner]]
-    columns += [rounded(d_enc[:, D // 3 : D // 3 + 3 * WIDTH]), late[:, :wide]]
+    columns = [late[:, down : down + inner], late[:, :wide]]
     columns = jnp.concatenate(columns, axis=1).reshape(WAYS, own, -1)
     columns = exchange_over_x(place, columns)
     columns_here = columns
@@ -1741,7 +1741,7 @@
             ((4, own), F32),
             ((2, ff_own), F32),
         ],
-        [columns, turned_out, late, d_ffn_dec],
+        [columns, early, turned_out, late, d_ffn_dec],
         2.0,
     )
     sums = sums + sum(shift_z(sums, k, depth) for k in range(1, depth))

time: 461 us -> 451 us (0.978)
  Pallas kernels: 88.6 us -> 76.9 us
  local copies, waits for them, and re-layouts: 77.7 us -> 68.3 us
    pallas_call x26, Pallas kernels: 88.6 us -> 76.9 us  [call(): pl.pallas_call(bring_in, grid=(1,) if windows else (), out_shape=shapes,...]
    unnamed x268 -> x304, local copies, waits for them, and re-layouts: 52.4 us -> 43.4 us
    ppermute x44 -> x49, waiting for transfers between devices: 150 us -> 151 us  [swap(): return lax.ppermute(values, axis, [(0, 1), (1, 0)])]
    ppermute x44 -> x49, starting transfers between devices: 40 us -> 40.3 us  [swap(): return lax.ppermute(values, axis, [(0, 1), (1, 0)])]
  transfers between devices with their start and end apart: 62 -> 67, of which waited for: 38 -> 45; matrix products, arithmetic and copies ran while one was open for 10% -> 9% of each run, Pallas kernels for 14% -> 13%
where the time goes in v1:
time: 451 us; the launch traced here: 445 us
  waiting for transfers between devices  191 us (42%)
  Pallas kernels  76.9 us (17%)
  local copies, waits for them, and re-layouts  68.3 us (15%)
  starting transfers between devices  63.9 us (14%)
  other arithmetic  26.6 us (6%)
  between operations  16.6 us (4%)
    ppermute x49, waiting for transfers between devices, swap(): return lax.ppermute(values, axis, [(0, 1), (1, 0)])  151 us
    pallas_call x26, Pallas kernels, call(): pl.pallas_call(bring_in, grid=(1,) if windows else (), out_shape=shapes,...  76.9 us
    unnamed x304, local copies, waits for them, and re-layouts  43.4 us
    ppermute x49, starting transfers between devices, swap(): return lax.ppermute(values, axis, [(0, 1), (1, 0)])  40.3 us
    ppermute x12, starting transfers between devices, shift_z(): lax.ppermute(values, 'dp', [(i, (i + hops) % count) for i in range(count)])  21.9 us
    all_gather x2, waiting for transfers between devices, gather(): return lax.all_gather(piece, ('dp', 'y'), axis=0, tiled=True)  20.9 us
    ppermute x12, waiting for transfers between devices, shift_z(): lax.ppermute(values, 'dp', [(i, (i + hops) % count) for i in range(count)])  17.8 us
  transfers between devices with their start and end apart: 67, of which 45 were waited for; matrix products, arithmetic and copies ran while one was open for 9% of the time, Pallas kernels for 13%

profile of v1, /device:TPU:0, one launch (start us, length us, event | category | flops | bytes accessed | tf_op | source)
XLA Modules:
  0.0 444.7 jit_solution(17193468179462492755)
XLA Ops:
  11.3 3.0 collective-permute-start.2
  15.0 5.8 %collective-permute-done.2 = bf16[2,24,2816]{2,1,0:T(8,128)(2,1)S(1)} collective-permute-done((bf16[2,24,2816]{2,1,0:T(8,128)(2,1)S(1)}, bf16[2,24,2816]{2,1,0:T(8,128)(2,1)S(1)}, u32[]{:S(2)}, u32[]{:S(2)}) %collective-permute-start.2) | collective-permute-done | bytes 270368 | tf_op jit(solution)/shard_map/ppermute | solution.py:705
  30.6 2.9 collective-permute-start.6
  36.0 14.9 %collective-permute-done.6 = bf16[96,896]{1,0:T(8,128)(2,1)S(1)} collective-permute-done((bf16[96,896]{1,0:T(8,128)(2,1)S(1)}, bf16[96,896]{1,0:T(8,128)(2,1)S(1)}, u32[]{:S(2)}, u32[]{:S(2)}) %collective-permute-start.6) | collective-permute-done | bytes 172064 | tf_op jit(solution)/shard_map/ppermute | solution.py:709
  54.3 13.9 %collective-permute-done.8 = bf16[4,96,896]{2,1,0:T(8,128)(2,1)S(1)} collective-permute-done((bf16[4,96,896]{2,1,0:T(8,128)(2,1)S(1)}, bf16[4,96,896]{2,1,0:T(8,128)(2,1)S(1)}, u32[]{:S(2)}, u32[]{:S(2)}) %collective-permute-start.8) | collective-permute-done | bytes 688160 | tf_op jit(solution)/shard_map/ppermute | solution.py:705
  77.3 5.2 %enc_attend.1 = (f32[2,256,192]{2,1,0:T(8,128)S(1)}, bf16[6,256,512]{2,1,0:T(8,128)(2,1)S(1)}, f32[256,768]{1,0:T(8,128)S(1)}, bf16[256,768]{1,0:T(8,128)(2,1)S(1)}) custom-call(s32[2]{0:T(128)S(1)} %pad_add_fusion.refs_0_, bf16[2,256,192]{2,1,0:T(8,128)(2,1)S(1)} %get-tuple-element.144.refs_1_.refs_8_, ...), custom_call_target="tpu_custom_call" | custom-call | flops 55000000 | bytes 148224 | tf_op jit(solution)/shard_map/enc_attend/pallas_call | solution.py:833
  88.1 8.8 %collective-permute-done.11.refs_2_ = bf16[256,768]{1,0:T(8,128)(2,1)S(1)} collective-permute-done((bf16[256,768]{1,0:T(8,128)(2,1)S(1)}, bf16[256,768]{1,0:T(8,128)(2,1)S(1)}, u32[]{:S(2)}, u32[]{:S(2)}) %collective-permute-start.11) | collective-permute-done | bytes 393248 | tf_op jit(solution)/shard_map/ppermute | solution.py:705
  97.6 20.2 %all-gather.3.cloned.1.call-done = bf16[768,3072]{1,0:T(8,128)(2,1)} async-done(((bf16[96,3072]{1,0:T(8,128)(2,1)}), bf16[768,3072]{1,0:T(8,128)(2,1)}) %all-gather.3.cloned.1.call-update) | async-done | bytes 4718608 | tf_op jit(solution)/shard_map/all_gather | solution.py:1504
  129.1 5.3 %dec_attend.1 = (f32[2,256,192]{2,1,0:T(8,128)S(1)}, bf16[6,256,512]{2,1,0:T(8,128)(2,1)S(1)}, f32[256,768]{1,0:T(8,128)S(1)}, bf16[256,768]{1,0:T(8,128)(2,1)S(1)}) custom-call(s32[2]{0:T(128)S(1)} %pad_add_fusion.1.refs_0_, bf16[2,256,192]{2,1,0:T(8,128)(2,1)S(1)} %get-tuple-element.149.refs_1_.refs_8_, ...), custom_call_target="tpu_custom_call" | custom-call | flops 55000000 | bytes 166656 | tf_op jit(solution)/shard_map/dec_attend/pallas_call | solution.py:833
  136.3 3.1 collective-permute-start.16
  142.7 6.6 %collective-permute-done.16.refs_2_ = bf16[256,768]{1,0:T(8,128)(2,1)S(1)} collective-permute-done((bf16[256,768]{1,0:T(8,128)(2,1)S(1)}, bf16[256,768]{1,0:T(8,128)(2,1)S(1)}, u32[]{:S(2)}, u32[]{:S(2)}) %collective-permute-start.16) | collective-permute-done | bytes 393248 | tf_op jit(solution)/shard_map/ppermute | solution.py:705
  151.0 6.3 %collective-permute-done.15.refs_2_ = bf16[256,768]{1,0:T(8,128)(2,1)S(1)} collective-permute-done((bf16[256,768]{1,0:T(8,128)(2,1)S(1)}, bf16[256,768]{1,0:T(8,128)(2,1)S(1)}, u32[]{:S(2)}, u32[]{:S(2)}) %collective-permute-start.15) | collective-permute-done | bytes 393248 | tf_op jit(solution)/shard_map/ppermute | solution.py:705
  161.4 3.7 cross_attend.1
  172.5 10.3 %collective-permute-done.18.refs_2_ = bf16[256,768]{1,0:T(8,128)(2,1)S(1)} collective-permute-done((bf16[256,768]{1,0:T(8,128)(2,1)}, bf16[256,768]{1,0:T(8,128)(2,1)S(1)}, u32[]{:S(2)}, u32[]{:S(2)}) %collective-permute-start.18) | collective-permute-done | bytes 393248 | tf_op jit(solution)/shard_map/ppermute | solution.py:705
  187.4 12.0 %dec_ffn.1 = (f32[256,768]{1,0:T(8,128)S(1)}, bf16[256,768]{1,0:T(8,128)(2,1)S(1)}, f32[2,256,1024]{2,1,0:T(8,128)S(1)}, bf16[2,256,512]{2,1,0:T(8,128)(2,1)S(1)...) custom-call(f32[256,768]{1,0:T(8,128)S(1)} %copy-done.28, f32[256,768]{1,0:T(8,128)S(1)} %copy-done.83, ...), custom_call_target="tpu_custom_call" | custom-call | flops 30000000 | bytes 365216 | tf_op jit(solution)/shard_map/dec_ffn/pallas_call | solution.py:833
  201.0 9.2 %collective-permute-done.22.refs_2_ = bf16[256,768]{1,0:T(8,128)(2,1)S(1)} collective-permute-done((bf16[256,768]{1,0:T(8,128)(2,1)S(1)}, bf16[256,768]{1,0:T(8,128)(2,1)S(1)}, u32[]{:S(2)}, u32[]{:S(2)}) %collective-permute-start.22) | collective-permute-done | bytes 393248 | tf_op jit(solution)/shard_map/ppermute | solution.py:705
  216.0 3.0 collective-permute-done.24
  221.1 4.8 %collective-permute-done.23.refs_4_ = bf16[256,768]{1,0:T(8,128)(2,1)S(1)} collective-permute-done((bf16[256,768]{1,0:T(8,128)(2,1)S(1)}, bf16[256,768]{1,0:T(8,128)(2,1)S(1)}, u32[]{:S(2)}, u32[]{:S(2)}) %collective-permute-start.23) | collective-permute-done | bytes 393248 | tf_op jit(solution)/shard_map/ppermute | solution.py:705
  237.5 5.4 %cross_attend_back.1 = (f32[256,768]{1,0:T(8,128)S(1)}, f32[1,768]{1,0:T(1,128)S(1)}, bf16[256,768]{1,0:T(8,128)(2,1)S(1)}, bf16[2,256,192]{2,1,0:T(8,128)(2,1)S...) custom-call(s32[2]{0:T(128)S(1)} %pad_add_fusion.refs_0_, f32[256,768]{1,0:T(8,128)S(1)} %copy-done.93, ...), custom_call_target="tpu_custom_call" | custom-call | flops 60000000 | bytes 295680 | tf_op jit(solution)/shard_map/cross_attend_back/pallas_call | solution.py:833
  247.9 9.9 %collective-permute-done.26.refs_2_ = bf16[256,768]{1,0:T(8,128)(2,1)S(1)} collective-permute-done((bf16[256,768]{1,0:T(8,128)(2,1)S(1)}, bf16[256,768]{1,0:T(8,128)(2,1)S(1)}, u32[]{:S(2)}, u32[]{:S(2)}) %collective-permute-start.26) | collective-permute-done | bytes 393248 | tf_op jit(solution)/shard_map/ppermute | solution.py:705
  257.8 7.6 %collective-permute-done.27.refs_4_ = bf16[256,768]{1,0:T(8,128)(2,1)S(1)} collective-permute-done((bf16[256,768]{1,0:T(8,128)(2,1)S(1)}, bf16[256,768]{1,0:T(8,128)(2,1)S(1)}, u32[]{:S(2)}, u32[]{:S(2)}) %collective-permute-start.27) | collective-permute-done | bytes 393248 | tf_op jit(solution)/shard_map/ppermute | solution.py:705
  272.1 9.7 %dec_attend_back.1 = (f32[256,768]{1,0:T(8,128)S(1)}, f32[1,768]{1,0:T(1,128)S(1)}, bf16[256,768]{1,0:T(8,128)(2,1)S(1)}, bf16[2,256,192]{2,1,0:T(8,128)(2,1)S(1...) custom-call(s32[2]{0:T(128)S(1)} %copy-done.116, ...), custom_call_target="tpu_custom_call" | custom-call | flops 90000000 | bytes 296448 | tf_op jit(solution)/shard_map/dec_attend_back/pallas_call | solution.py:833
  300.7 8.6 %collective-permute-done.28.refs_4_ = bf16[256,768]{1,0:T(8,128)(2,1)S(1)} collective-permute-done((bf16[256,768]{1,0:T(8,128)(2,1)}, bf16[256,768]{1,0:T(8,128)(2,1)S(1)}, u32[]{:S(2)}, u32[]{:S(2)}) %collective-permute-start.28) | collective-permute-done | bytes 393248 | tf_op jit(solution)/shard_map/ppermute | solution.py:705
  313.1 9.4 %enc_attend_back.1 = (f32[256,768]{1,0:T(8,128)S(1)}, f32[1,768]{1,0:T(1,128)S(1)}, bf16[256,768]{1,0:T(8,128)(2,1)S(1)}, bf16[2,256,192]{2,1,0:T(8,128)(2,1)S(1...) custom-call(s32[2]{0:T(128)S(1)} %pad_add_fusion.refs_0_, ...), custom_call_target="tpu_custom_call" | custom-call | flops 90000000 | bytes 278016 | tf_op jit(solution)/shard_map/enc_attend_back/pallas_call | solution.py:833
  341.9 6.9 %collective-permute-done.32.refs_3_ = bf16[256,768]{1,0:T(8,128)(2,1)} collective-permute-done((bf16[256,768]{1,0:T(8,128)(2,1)}, bf16[256,768]{1,0:T(8,128)(2,1)}, u32[]{:S(2)}, u32[]{:S(2)}) %collective-permute-start.32) | collective-permute-done | bytes 393248 | tf_op jit(solution)/shard_map/ppermute | solution.py:705
  350.4 5.7 %collective-permute-done.31.refs_3_ = bf16[256,768]{1,0:T(8,128)(2,1)S(1)} collective-permute-done((bf16[256,768]{1,0:T(8,128)(2,1)}, bf16[256,768]{1,0:T(8,128)(2,1)S(1)}, u32[]{:S(2)}, u32[]{:S(2)}) %collective-permute-start.31) | collective-permute-done | bytes 393248 | tf_op jit(solution)/shard_map/ppermute | solution.py:705
  356.5 3.1 collective-permute-done.35
  371.1 2.8 collective-permute-done.53
  383.5 9.3 %collective-permute-done.37 = bf16[64,768]{1,0:T(8,128)(2,1)S(1)} collective-permute-done((bf16[64,768]{1,0:T(8,128)(2,1)S(1)}, bf16[64,768]{1,0:T(8,128)(2,1)S(1)}, u32[]{:S(2)}, u32[]{:S(2)}) %collective-permute-start.37) | collective-permute-done | bytes 98336 | tf_op jit(solution)/shard_map/ppermute | solution.py:705
  395.4 2.7 collective-permute-done.36
  413.9 3.0 collective-permute-start.58
  434.5 2.8 shards.1
  (638 shorter events, 202.0 us)
Async XLA Ops:
  7.2 110.6 %all-gather.3.cloned.1.call-start = ((), (), s32[]{:S(2)}) async-start(), calls=%async_computation.2 | async-start | bytes 5308416 | tf_op jit(solution)/shard_map/all_gather | solution.py:1504
  11.3 9.5 %collective-permute-start.2 = (bf16[2,24,2816]{2,1,0:T(8,128)(2,1)S(1)}, bf16[2,24,2816]{2,1,0:T(8,128)(2,1)S(1)}, u32[]{:S(2)}, u32[]{:S(2)}) collective-permute-start(bf16[2,24,2816]{2,1,0:T(8,128)(2,1)S(1)} %dynamic-slice_bitcast_fusion), channel_id=1, source_target_pairs={{0,2},{2,0},{1,3},{3,1},{4,6},{6,4},{5,7},{7,5},{8,10},{10,8},{9,1... | collective-permute-start | bytes 811016 | tf_op jit(solution)/shard_map/ppermute | solution.py:705
  23.6 147.5 %all-gather.5.cloned.1.call-start = ((), (), s32[]{:S(2)}) async-start(), calls=%async_computation.3 | async-start | bytes 2654208 | tf_op jit(solution)/shard_map/all_gather | solution.py:1504
  24.1 28.5 %collective-permute-start = (bf16[4,64,768]{2,1,0:T(8,128)(2,1)S(1)}, bf16[4,64,768]{2,1,0:T(8,128)(2,1)S(1)}, u32[]{:S(2)}, u32[]{:S(2)}) collective-permute-start(bf16[4,64,768]{2,1,0:T(8,128)(2,1)S(1)} %pad_maximum_fusion.9), channel_id=1, source_target_pairs={{0,4},{4,0},{1,5},{5,1},{2,6},{6,2},{3,7},{7,3},{8,12},{12,8},{9,1... | collective-permute-start | bytes 1179656 | tf_op jit(solution)/shard_map/ppermute | solution.py:705
  26.3 9.6 %collective-permute-start.5 = (bf16[96,896]{1,0:T(8,128)(2,1)S(1)}, bf16[96,896]{1,0:T(8,128)(2,1)S(1)}, u32[]{:S(2)}, u32[]{:S(2)}) collective-permute-start(bf16[96,896]{1,0:T(8,128)(2,1)S(1)} %fusion.25), channel_id=1, source_target_pairs={{0,8},{8,16},{16,24},{24,0},{1,9},{9,17},{17,25},{25,1},{2,10},{10... | collective-permute-start | bytes 516104 | tf_op jit(solution)/shard_map/ppermute | solution.py:709
  30.6 20.3 %collective-permute-start.6 = (bf16[96,896]{1,0:T(8,128)(2,1)S(1)}, bf16[96,896]{1,0:T(8,128)(2,1)S(1)}, u32[]{:S(2)}, u32[]{:S(2)}) collective-permute-start(bf16[96,896]{1,0:T(8,128)(2,1)S(1)} %fusion.25), channel_id=1, source_target_pairs={{0,16},{8,24},{16,0},{24,8},{1,17},{9,25},{17,1},{25,9},{2,18},{10... | collective-permute-start | bytes 516104 | tf_op jit(solution)/shard_map/ppermute | solution.py:709
  33.5 17.4 %collective-permute-start.7 = (bf16[96,896]{1,0:T(8,128)(2,1)S(1)}, bf16[96,896]{1,0:T(8,128)(2,1)S(1)}, u32[]{:S(2)}, u32[]{:S(2)}) collective-permute-start(bf16[96,896]{1,0:T(8,128)(2,1)S(1)} %fusion.25), channel_id=1, source_target_pairs={{0,24},{8,0},{16,8},{24,16},{1,25},{9,1},{17,9},{25,17},{2,26},{10... | collective-permute-start | bytes 516104 | tf_op jit(solution)/shard_map/ppermute | solution.py:709
  51.0 17.2 %collective-permute-start.8 = (bf16[4,96,896]{2,1,0:T(8,128)(2,1)S(1)}, bf16[4,96,896]{2,1,0:T(8,128)(2,1)S(1)}, u32[]{:S(2)}, u32[]{:S(2)}) collective-permute-start(bf16[4,96,896]{2,1,0:T(8,128)(2,1)S(1)} %bitcast_dynamic-update-slice_fusion), channel_id=1, source_target_pairs={{0,4},{4,0},{1,5},{5,1},{2,6},{6,2},{3,7},{7,3},{8,12},{12,8},{9,1... | collective-permute-start | bytes 2064392 | tf_op jit(solution)/shard_map/ppermute | solution.py:705
  52.8 19.0 %collective-permute-start.1 = (bf16[2,4,64,768]{3,2,1,0:T(8,128)(2,1)S(1)}, bf16[2,4,64,768]{3,2,1,0:T(8,128)(2,1)S(1)}, u32[]{:S(2)}, u32[]{:S(2)}) collective-permute-start(bf16[2,4,64,768]{3,2,1,0:T(8,128)(2,1)S(1)} %pad_maximum_fusion.1), channel_id=1, source_target_pairs={{0,2},{2,0},{1,3},{3,1},{4,6},{6,4},{5,7},{7,5},{8,10},{10,8},{9,1... | collective-permute-start | bytes 2359304 | tf_op jit(solution)/shard_map/ppermute | solution.py:705
  75.8 11.1 %collective-permute-start.20 = (bf16[2,24,1024]{2,1,0:T(8,128)(2,1)S(1)}, bf16[2,24,1024]{2,1,0:T(8,128)(2,1)S(1)}, u32[]{:S(2)}, u32[]{:S(2)}) collective-permute-start(bf16[2,24,1024]{2,1,0:T(8,128)(2,1)S(1)} %fusion.35), channel_id=1, source_target_pairs={{0,1},{1,0},{2,3},{3,2},{4,5},{5,4},{6,7},{7,6},{8,9},{9,8},{10,11... | collective-permute-start | bytes 294920 | tf_op jit(solution)/shard_map/ppermute | solution.py:705
  85.4 11.5 %collective-permute-start.11 = (bf16[256,768]{1,0:T(8,128)(2,1)S(1)}, bf16[256,768]{1,0:T(8,128)(2,1)S(1)}, u32[]{:S(2)}, u32[]{:S(2)}) collective-permute-start(bf16[256,768]{1,0:T(8,128)(2,1)S(1)} %get-tuple-element.147), channel_id=1, source_target_pairs={{0,2},{2,0},{1,3},{3,1},{4,6},{6,4},{5,7},{7,5},{8,10},{10,8},{9,1... | collective-permute-start | bytes 1179656 | tf_op jit(solution)/shard_map/ppermute | solution.py:705
  87.8 206.7 %reduce-scatter.3.cloned.1.call-start = ((), (), s32[]{:S(2)}) async-start(), calls=%async_computation.4 | async-start | bytes 2654208 | tf_op jit(solution)/shard_map/reduce_scatter | solution.py:1596
  120.6 18.8 %collective-permute-start.14 = (bf16[768,1536]{1,0:T(8,128)(2,1)S(1)}, bf16[768,1536]{1,0:T(8,128)(2,1)S(1)}, u32[]{:S(2)}, u32[]{:S(2)}) collective-permute-start(bf16[768,1536]{1,0:T(8,128)(2,1)S(1)} %get-tuple-element.310.refs_4_.refs_6_), channel_id=1, source_target_pairs={{0,1},{1,0},{2,3},{3,2},{4,5},{5,4},{6,7},{7,6},{8,9},{9,8},{10,11... | collective-permute-start | bytes 7077896 | tf_op jit(solution)/shard_map/ppermute | solution.py:705
  136.3 13.0 %collective-permute-start.16 = (bf16[256,768]{1,0:T(8,128)(2,1)S(1)}, bf16[256,768]{1,0:T(8,128)(2,1)S(1)}, u32[]{:S(2)}, u32[]{:S(2)}) collective-permute-start(bf16[256,768]{1,0:T(8,128)(2,1)S(1)} %get-tuple-element.151), channel_id=1, source_target_pairs={{0,2},{2,0},{1,3},{3,1},{4,6},{6,4},{5,7},{7,5},{8,10},{10,8},{9,1... | collective-permute-start | bytes 1179656 | tf_op jit(solution)/shard_map/ppermute | solution.py:705
  142.7 14.6 %collective-permute-start.15 = (bf16[256,768]{1,0:T(8,128)(2,1)S(1)}, bf16[256,768]{1,0:T(8,128)(2,1)S(1)}, u32[]{:S(2)}, u32[]{:S(2)}) collective-permute-start(bf16[256,768]{1,0:T(8,128)(2,1)S(1)} %get-tuple-element.155), channel_id=1, source_target_pairs={{0,2},{2,0},{1,3},{3,1},{4,6},{6,4},{5,7},{7,5},{8,10},{10,8},{9,1... | collective-permute-start | bytes 1179656 | tf_op jit(solution)/shard_map/ppermute | solution.py:705
  171.0 11.7 %collective-permute-start.21 = (bf16[768,1536]{1,0:T(8,128)(2,1)}, bf16[768,1536]{1,0:T(8,128)(2,1)S(1)}, u32[]{:S(2)}, u32[]{:S(2)}) collective-permute-start(bf16[768,1536]{1,0:T(8,128)(2,1)} %all-gather.5.cloned.1.call-done.refs_4_.refs_6_), channel_id=1, source_target_pairs={{0,1},{1,0},{2,3},{3,2},{4,5},{5,4},{6,7},{7,6},{8,9},{9,8},{10,11... | collective-permute-start | bytes 7077896 | tf_op jit(solution)/shard_map/ppermute | solution.py:705
  171.0 11.7 %collective-permute-start.18 = (bf16[256,768]{1,0:T(8,128)(2,1)}, bf16[256,768]{1,0:T(8,128)(2,1)S(1)}, u32[]{:S(2)}, u32[]{:S(2)}) collective-permute-start(bf16[256,768]{1,0:T(8,128)(2,1)} %copy-done.118), channel_id=1, source_target_pairs={{0,2},{2,0},{1,3},{3,1},{4,6},{6,4},{5,7},{7,5},{8,10},{10,8},{9,1... | collective-permute-start | bytes 1179656 | tf_op jit(solution)/shard_map/ppermute | solution.py:705
  199.4 10.8 %collective-permute-start.22 = (bf16[256,768]{1,0:T(8,128)(2,1)S(1)}, bf16[256,768]{1,0:T(8,128)(2,1)S(1)}, u32[]{:S(2)}, u32[]{:S(2)}) collective-permute-start(bf16[256,768]{1,0:T(8,128)(2,1)S(1)} %get-tuple-element.169), channel_id=1, source_target_pairs={{0,2},{2,0},{1,3},{3,1},{4,6},{6,4},{5,7},{7,5},{8,10},{10,8},{9,1... | collective-permute-start | bytes 1179656 | tf_op jit(solution)/shard_map/ppermute | solution.py:705
  214.5 11.5 %collective-permute-start.23 = (bf16[256,768]{1,0:T(8,128)(2,1)S(1)}, bf16[256,768]{1,0:T(8,128)(2,1)S(1)}, u32[]{:S(2)}, u32[]{:S(2)}) collective-permute-start(bf16[256,768]{1,0:T(8,128)(2,1)S(1)} %get-tuple-element.175), channel_id=1, source_target_pairs={{0,2},{2,0},{1,3},{3,1},{4,6},{6,4},{5,7},{7,5},{8,10},{10,8},{9,1... | collective-permute-start | bytes 1179656 | tf_op jit(solution)/shard_map/ppermute | solution.py:705
  226.8 182.1 %reduce-scatter.5.cloned.1.call-start = ((), (), s32[]{:S(2)}) async-start(), calls=%async_computation.5 | async-start | bytes 5308416 | tf_op jit(solution)/shard_map/reduce_scatter | solution.py:1596
  245.8 12.0 %collective-permute-start.26 = (bf16[256,768]{1,0:T(8,128)(2,1)S(1)}, bf16[256,768]{1,0:T(8,128)(2,1)S(1)}, u32[]{:S(2)}, u32[]{:S(2)}) collective-permute-start(bf16[256,768]{1,0:T(8,128)(2,1)S(1)} %get-tuple-element.189), channel_id=1, source_target_pairs={{0,2},{2,0},{1,3},{3,1},{4,6},{6,4},{5,7},{7,5},{8,10},{10,8},{9,1... | collective-permute-start | bytes 1179656 | tf_op jit(solution)/shard_map/ppermute | solution.py:705
  247.2 18.2 %collective-permute-start.27 = (bf16[256,768]{1,0:T(8,128)(2,1)S(1)}, bf16[256,768]{1,0:T(8,128)(2,1)S(1)}, u32[]{:S(2)}, u32[]{:S(2)}) collective-permute-start(bf16[256,768]{1,0:T(8,128)(2,1)S(1)} %get-tuple-element.190), channel_id=1, source_target_pairs={{0,2},{2,0},{1,3},{3,1},{4,6},{6,4},{5,7},{7,5},{8,10},{10,8},{9,1... | collective-permute-start | bytes 1179656 | tf_op jit(solution)/shard_map/ppermute | solution.py:705
  272.0 18.6 %collective-permute-start.40 = (bf16[768,1536]{1,0:T(8,128)(2,1)S(1)}, bf16[768,1536]{1,0:T(8,128)(2,1)S(1)}, u32[]{:S(2)}, u32[]{:S(2)}) collective-permute-start(bf16[768,1536]{1,0:T(8,128)(2,1)S(1)} %get-tuple-element.203), channel_id=1, source_target_pairs={{0,1},{1,0},{2,3},{3,2},{4,5},{5,4},{6,7},{7,6},{8,9},{9,8},{10,11... | collective-permute-start | bytes 7077896 | tf_op jit(solution)/shard_map/ppermute | solution.py:705
  299.2 10.1 %collective-permute-start.28 = (bf16[256,768]{1,0:T(8,128)(2,1)}, bf16[256,768]{1,0:T(8,128)(2,1)S(1)}, u32[]{:S(2)}, u32[]{:S(2)}) collective-permute-start(bf16[256,768]{1,0:T(8,128)(2,1)} %copy-done.117), channel_id=1, source_target_pairs={{0,2},{2,0},{1,3},{3,1},{4,6},{6,4},{5,7},{7,5},{8,10},{10,8},{9,1... | collective-permute-start | bytes 1179656 | tf_op jit(solution)/shard_map/ppermute | solution.py:705
  335.5 24.1 %collective-permute-start.35 = (bf16[4,96,896]{2,1,0:T(8,128)(2,1)}, bf16[4,96,896]{2,1,0:T(8,128)(2,1)}, u32[]{:S(2)}, u32[]{:S(2)}) collective-permute-start(bf16[4,96,896]{2,1,0:T(8,128)(2,1)} %fusion.1), channel_id=1, source_target_pairs={{0,4},{4,0},{1,5},{5,1},{2,6},{6,2},{3,7},{7,3},{8,12},{12,8},{9,1... | collective-permute-start | bytes 2064392 | tf_op jit(solution)/shard_map/ppermute | solution.py:705
  336.5 12.3 %collective-permute-start.32 = (bf16[256,768]{1,0:T(8,128)(2,1)}, bf16[256,768]{1,0:T(8,128)(2,1)}, u32[]{:S(2)}, u32[]{:S(2)}) collective-permute-start(bf16[256,768]{1,0:T(8,128)(2,1)} %get-tuple-element.230), channel_id=1, source_target_pairs={{0,2},{2,0},{1,3},{3,1},{4,6},{6,4},{5,7},{7,5},{8,10},{10,8},{9,1... | collective-permute-start | bytes 1179656 | tf_op jit(solution)/shard_map/ppermute | solution.py:705
  338.0 18.0 %collective-permute-start.31 = (bf16[256,768]{1,0:T(8,128)(2,1)}, bf16[256,768]{1,0:T(8,128)(2,1)S(1)}, u32[]{:S(2)}, u32[]{:S(2)}) collective-permute-start(bf16[256,768]{1,0:T(8,128)(2,1)} %get-tuple-element.220), channel_id=1, source_target_pairs={{0,2},{2,0},{1,3},{3,1},{4,6},{6,4},{5,7},{7,5},{8,10},{10,8},{9,1... | collective-permute-start | bytes 1179656 | tf_op jit(solution)/shard_map/ppermute | solution.py:705
  362.1 38.5 %collective-permute-start.43 = (bf16[96,896]{1,0:T(8,128)(2,1)S(1)}, bf16[96,896]{1,0:T(8,128)(2,1)S(1)}, u32[]{:S(2)}, u32[]{:S(2)}) collective-permute-start(bf16[96,896]{1,0:T(8,128)(2,1)S(1)} %get-tuple-element.330), channel_id=1, source_target_pairs={{0,8},{8,16},{16,24},{24,0},{1,9},{9,17},{17,25},{25,1},{2,10},{10... | collective-permute-start | bytes 516104 | tf_op jit(solution)/shard_map/ppermute | solution.py:709
  363.5 37.1 %collective-permute-start.44 = (bf16[96,896]{1,0:T(8,128)(2,1)S(1)}, bf16[96,896]{1,0:T(8,128)(2,1)S(1)}, u32[]{:S(2)}, u32[]{:S(2)}) collective-permute-start(bf16[96,896]{1,0:T(8,128)(2,1)S(1)} %get-tuple-element.332), channel_id=1, source_target_pairs={{0,16},{8,24},{16,0},{24,8},{1,17},{9,25},{17,1},{25,9},{2,18},{10... | collective-permute-start | bytes 516104 | tf_op jit(solution)/shard_map/ppermute | solution.py:709
  379.6 20.9 %collective-permute-start.45 = (bf16[96,896]{1,0:T(8,128)(2,1)S(1)}, bf16[96,896]{1,0:T(8,128)(2,1)S(1)}, u32[]{:S(2)}, u32[]{:S(2)}) collective-permute-start(bf16[96,896]{1,0:T(8,128)(2,1)S(1)} %get-tuple-element.331), channel_id=1, source_target_pairs={{0,24},{8,0},{16,8},{24,16},{1,25},{9,1},{17,9},{25,17},{2,26},{10... | collective-permute-start | bytes 516104 | tf_op jit(solution)/shard_map/ppermute | solution.py:709
  381.5 22.2 %collective-permute-start.39 = (f32[64,768]{1,0:T(8,128)}, f32[64,768]{1,0:T(8,128)}, u32[]{:S(2)}, u32[]{:S(2)}) collective-permute-start(f32[64,768]{1,0:T(8,128)} %dynamic-slice_bitcast_fusion.2), channel_id=1, source_target_pairs={{0,4},{4,0},{1,5},{5,1},{2,6},{6,2},{3,7},{7,3},{8,12},{12,8},{9,1... | collective-permute-start | bytes 589832 | tf_op jit(solution)/shard_map/ppermute | solution.py:705
  382.1 10.7 %collective-permute-start.37 = (bf16[64,768]{1,0:T(8,128)(2,1)S(1)}, bf16[64,768]{1,0:T(8,128)(2,1)S(1)}, u32[]{:S(2)}, u32[]{:S(2)}) collective-permute-start(bf16[64,768]{1,0:T(8,128)(2,1)S(1)} %dynamic-slice_bitcast_fusion.8), channel_id=1, source_target_pairs={{0,4},{4,0},{1,5},{5,1},{2,6},{6,2},{3,7},{7,3},{8,12},{12,8},{9,1... | collective-permute-start | bytes 294920 | tf_op jit(solution)/shard_map/ppermute | solution.py:705
  (185 other events, 1240.0 us)
Sparse Core Ops, SparseCore 0:
  23.7 94.1 all-gather.2
  120.0 50.9 all-gather.4
  226.9 67.4 reduce-scatter.2
  299.3 104.4 reduce-scatter.4

commit v2 on v1

--- a/solution.py
+++ b/solution.py
@@ -1293,14 +1293,14 @@
             size = min(128, values.shape[1] - k)
             out_ref[at + k // 128 : at + k // 128 + 1, :size] = values[:, k : k + size]
 
-    put(0, line(squares(late_ref[:, :wide], D)))
+    put(0, line(squares(late_ref[:, inner : inner + wide], D)))
     put(wide // 128, line(squares(dec_ref[:, :wide], D)))
     at = 2 * wide // 128
-    put(at, line(squares(late_ref[:, width : width + inner], D)))
+    put(at, line(squares(late_ref[:, :inner], D)))
     put(at + inner // 128, line(squares(self_ref[:, third : third + 3 * WIDTH], D)))
     at = 30
-    for ref in (late_ref, dec_ref):
-        down = squares(ref[:, wide:width], FF)
+    for ref, begin in ((late_ref, inner), (dec_ref, 0)):
+        down = squares(ref[:, begin + wide : begin + width], FF)
         put(at, line(down[:rows]))
         put(at + 2 * third // 128, line(down[rows:, :third]) + line(down[rows:, third:]))
         at += D // 128
@@ -1357,8 +1357,8 @@
                     piece = ref[q, :, first : first + ff_own]
                     hin_ref[layer, j, :, at : at + ff_own] = piece
             row_hin_ref[2 * layer + j : 2 * layer + j + 1, :] = half_mean_rows(hin_ref[layer, j])
-    for layer, ref in enumerate((late_ref, dec_ref)):
-        down = ref[:, wide:width].astype(F32)
+    for layer, (ref, begin) in enumerate(((late_ref, 6 * WIDTH), (dec_ref, 0))):
+        down = ref[:, begin + wide : begin + width].astype(F32)
         hout_ref[layer, :, : 2 * third] = down[:ff_own]
         half = ff_own // 2
         hout_ref[layer, :half, 2 * third :] = down[ff_own:, :third]
@@ -1683,7 +1683,7 @@
     d_out = both(d_out, d_out_sib)
     d_out = jnp.stack([turned_parts(d_out[k], depth) for k in range(2)], 1)
     d_in = d_in.astype(F32) + after(swap(d_in_sib, "c"), d_ffn_dec).astype(F32)
-    late = [blocks(d_ffn_enc), blocks(rounded(d_in)), pack_out(d_out)]
+    late = [blocks(rounded(d_in)), blocks(d_ffn_enc), pack_out(d_out)]
     late = scatter(jnp.concatenate(late, axis=2))
     got = after(swap(other, "c"), dkv_dec)
     dkv_enc, part, low = project_back(
@@ -1723,8 +1723,7 @@
     out_mine = unpack_out_piece(late[:, down + inner :])
     turned_out = jnp.concatenate([rounded(out_enc_mine.reshape(1, own, D)), out_mine])
     turned_out = turn(turned_out, depth).astype(F32)
-    columns = [late[:, down : down + inner], late[:, :wide]]
-    columns = jnp.concatenate(columns, axis=1).reshape(WAYS, own, -1)
+    columns = late[:, : inner + wide].reshape(WAYS, own, -1)
     columns = exchange_over_x(place, columns)
     columns_here = columns
     columns = exchange_over_cores(place, columns).astype(F32)

time: 451 us -> 450 us (level)
  no operation moved by 1% of the time
where the time goes in v2:
time: 450 us; the launch traced here: 444 us
  waiting for transfers between devices  191 us (42%)
  Pallas kernels  76.9 us (17%)
  local copies, waits for them, and re-layouts  67.4 us (15%)
  starting transfers between devices  63.9 us (14%)
  other arithmetic  26.6 us (6%)
  between operations  16.6 us (4%)
    ppermute x49, waiting for transfers between devices, swap(): return lax.ppermute(values, axis, [(0, 1), (1, 0)])  151 us
    pallas_call x26, Pallas kernels, call(): pl.pallas_call(bring_in, grid=(1,) if windows else (), out_shape=shapes,...  76.9 us
    unnamed x304, local copies, waits for them, and re-layouts  43.4 us
    ppermute x49, starting transfers between devices, swap(): return lax.ppermute(values, axis, [(0, 1), (1, 0)])  40.3 us
    ppermute x12, starting transfers between devices, shift_z(): lax.ppermute(values, 'dp', [(i, (i + hops) % count) for i in range(count)])  21.9 us
    all_gather x2, waiting for transfers between devices, gather(): return lax.all_gather(piece, ('dp', 'y'), axis=0, tiled=True)  20.9 us
    ppermute x12, waiting for transfers between devices, shift_z(): lax.ppermute(values, 'dp', [(i, (i + hops) % count) for i in range(count)])  17.8 us
  transfers between devices with their start and end apart: 67, of which 45 were waited for; matrix products, arithmetic and copies ran while one was open for 9% of the time, Pallas kernels for 13%

profile of v2, /device:TPU:0, one launch (start us, length us, event | category | flops | bytes accessed | tf_op | source)
XLA Modules:
  0.0 443.8 jit_solution(17495833073756853509)
XLA Ops:
  11.3 3.0 collective-permute-start.2
  15.0 5.8 %collective-permute-done.2 = bf16[2,24,2816]{2,1,0:T(8,128)(2,1)S(1)} collective-permute-done((bf16[2,24,2816]{2,1,0:T(8,128)(2,1)S(1)}, bf16[2,24,2816]{2,1,0:T(8,128)(2,1)S(1)}, u32[]{:S(2)}, u32[]{:S(2)}) %collective-permute-start.2) | collective-permute-done | bytes 270368 | tf_op jit(solution)/shard_map/ppermute | solution.py:705
  30.6 2.9 collective-permute-start.6
  36.0 14.9 %collective-permute-done.6 = bf16[96,896]{1,0:T(8,128)(2,1)S(1)} collective-permute-done((bf16[96,896]{1,0:T(8,128)(2,1)S(1)}, bf16[96,896]{1,0:T(8,128)(2,1)S(1)}, u32[]{:S(2)}, u32[]{:S(2)}) %collective-permute-start.6) | collective-permute-done | bytes 172064 | tf_op jit(solution)/shard_map/ppermute | solution.py:709
  54.3 13.9 %collective-permute-done.8 = bf16[4,96,896]{2,1,0:T(8,128)(2,1)S(1)} collective-permute-done((bf16[4,96,896]{2,1,0:T(8,128)(2,1)S(1)}, bf16[4,96,896]{2,1,0:T(8,128)(2,1)S(1)}, u32[]{:S(2)}, u32[]{:S(2)}) %collective-permute-start.8) | collective-permute-done | bytes 688160 | tf_op jit(solution)/shard_map/ppermute | solution.py:705
  77.3 5.2 %enc_attend.1 = (f32[2,256,192]{2,1,0:T(8,128)S(1)}, bf16[6,256,512]{2,1,0:T(8,128)(2,1)S(1)}, f32[256,768]{1,0:T(8,128)S(1)}, bf16[256,768]{1,0:T(8,128)(2,1)S(1)}) custom-call(s32[2]{0:T(128)S(1)} %pad_add_fusion.refs_0_, bf16[2,256,192]{2,1,0:T(8,128)(2,1)S(1)} %get-tuple-element.144.refs_1_.refs_8_, ...), custom_call_target="tpu_custom_call" | custom-call | flops 55000000 | bytes 148224 | tf_op jit(solution)/shard_map/enc_attend/pallas_call | solution.py:833
  88.1 8.8 %collective-permute-done.11.refs_2_ = bf16[256,768]{1,0:T(8,128)(2,1)S(1)} collective-permute-done((bf16[256,768]{1,0:T(8,128)(2,1)S(1)}, bf16[256,768]{1,0:T(8,128)(2,1)S(1)}, u32[]{:S(2)}, u32[]{:S(2)}) %collective-permute-start.11) | collective-permute-done | bytes 393248 | tf_op jit(solution)/shard_map/ppermute | solution.py:705
  97.6 20.2 %all-gather.3.cloned.1.call-done = bf16[768,3072]{1,0:T(8,128)(2,1)} async-done(((bf16[96,3072]{1,0:T(8,128)(2,1)}), bf16[768,3072]{1,0:T(8,128)(2,1)}) %all-gather.3.cloned.1.call-update) | async-done | bytes 4718608 | tf_op jit(solution)/shard_map/all_gather | solution.py:1504
  129.1 5.3 %dec_attend.1 = (f32[2,256,192]{2,1,0:T(8,128)S(1)}, bf16[6,256,512]{2,1,0:T(8,128)(2,1)S(1)}, f32[256,768]{1,0:T(8,128)S(1)}, bf16[256,768]{1,0:T(8,128)(2,1)S(1)}) custom-call(s32[2]{0:T(128)S(1)} %pad_add_fusion.1.refs_0_, bf16[2,256,192]{2,1,0:T(8,128)(2,1)S(1)} %get-tuple-element.149.refs_1_.refs_8_, ...), custom_call_target="tpu_custom_call" | custom-call | flops 55000000 | bytes 166656 | tf_op jit(solution)/shard_map/dec_attend/pallas_call | solution.py:833
  136.3 3.1 collective-permute-start.16
  142.7 6.6 %collective-permute-done.16.refs_2_ = bf16[256,768]{1,0:T(8,128)(2,1)S(1)} collective-permute-done((bf16[256,768]{1,0:T(8,128)(2,1)S(1)}, bf16[256,768]{1,0:T(8,128)(2,1)S(1)}, u32[]{:S(2)}, u32[]{:S(2)}) %collective-permute-start.16) | collective-permute-done | bytes 393248 | tf_op jit(solution)/shard_map/ppermute | solution.py:705
  151.0 6.3 %collective-permute-done.15.refs_2_ = bf16[256,768]{1,0:T(8,128)(2,1)S(1)} collective-permute-done((bf16[256,768]{1,0:T(8,128)(2,1)S(1)}, bf16[256,768]{1,0:T(8,128)(2,1)S(1)}, u32[]{:S(2)}, u32[]{:S(2)}) %collective-permute-start.15) | collective-permute-done | bytes 393248 | tf_op jit(solution)/shard_map/ppermute | solution.py:705
  161.4 3.7 cross_attend.1
  172.5 10.3 %collective-permute-done.18.refs_2_ = bf16[256,768]{1,0:T(8,128)(2,1)S(1)} collective-permute-done((bf16[256,768]{1,0:T(8,128)(2,1)}, bf16[256,768]{1,0:T(8,128)(2,1)S(1)}, u32[]{:S(2)}, u32[]{:S(2)}) %collective-permute-start.18) | collective-permute-done | bytes 393248 | tf_op jit(solution)/shard_map/ppermute | solution.py:705
  187.4 12.0 %dec_ffn.1 = (f32[256,768]{1,0:T(8,128)S(1)}, bf16[256,768]{1,0:T(8,128)(2,1)S(1)}, f32[2,256,1024]{2,1,0:T(8,128)S(1)}, bf16[2,256,512]{2,1,0:T(8,128)(2,1)S(1)...) custom-call(f32[256,768]{1,0:T(8,128)S(1)} %copy-done.28, f32[256,768]{1,0:T(8,128)S(1)} %copy-done.83, ...), custom_call_target="tpu_custom_call" | custom-call | flops 30000000 | bytes 365216 | tf_op jit(solution)/shard_map/dec_ffn/pallas_call | solution.py:833
  201.0 9.2 %collective-permute-done.22.refs_2_ = bf16[256,768]{1,0:T(8,128)(2,1)S(1)} collective-permute-done((bf16[256,768]{1,0:T(8,128)(2,1)S(1)}, bf16[256,768]{1,0:T(8,128)(2,1)S(1)}, u32[]{:S(2)}, u32[]{:S(2)}) %collective-permute-start.22) | collective-permute-done | bytes 393248 | tf_op jit(solution)/shard_map/ppermute | solution.py:705
  216.0 3.0 collective-permute-done.24
  221.1 4.8 %collective-permute-done.23.refs_4_ = bf16[256,768]{1,0:T(8,128)(2,1)S(1)} collective-permute-done((bf16[256,768]{1,0:T(8,128)(2,1)S(1)}, bf16[256,768]{1,0:T(8,128)(2,1)S(1)}, u32[]{:S(2)}, u32[]{:S(2)}) %collective-permute-start.23) | collective-permute-done | bytes 393248 | tf_op jit(solution)/shard_map/ppermute | solution.py:705
  237.5 5.4 %cross_attend_back.1 = (f32[256,768]{1,0:T(8,128)S(1)}, f32[1,768]{1,0:T(1,128)S(1)}, bf16[256,768]{1,0:T(8,128)(2,1)S(1)}, bf16[2,256,192]{2,1,0:T(8,128)(2,1)S...) custom-call(s32[2]{0:T(128)S(1)} %pad_add_fusion.refs_0_, f32[256,768]{1,0:T(8,128)S(1)} %copy-done.93, ...), custom_call_target="tpu_custom_call" | custom-call | flops 60000000 | bytes 295680 | tf_op jit(solution)/shard_map/cross_attend_back/pallas_call | solution.py:833
  247.9 9.9 %collective-permute-done.26.refs_2_ = bf16[256,768]{1,0:T(8,128)(2,1)S(1)} collective-permute-done((bf16[256,768]{1,0:T(8,128)(2,1)S(1)}, bf16[256,768]{1,0:T(8,128)(2,1)S(1)}, u32[]{:S(2)}, u32[]{:S(2)}) %collective-permute-start.26) | collective-permute-done | bytes 393248 | tf_op jit(solution)/shard_map/ppermute | solution.py:705
  257.8 7.6 %collective-permute-done.27.refs_4_ = bf16[256,768]{1,0:T(8,128)(2,1)S(1)} collective-permute-done((bf16[256,768]{1,0:T(8,128)(2,1)S(1)}, bf16[256,768]{1,0:T(8,128)(2,1)S(1)}, u32[]{:S(2)}, u32[]{:S(2)}) %collective-permute-start.27) | collective-permute-done | bytes 393248 | tf_op jit(solution)/shard_map/ppermute | solution.py:705
  272.1 9.7 %dec_attend_back.1 = (f32[256,768]{1,0:T(8,128)S(1)}, f32[1,768]{1,0:T(1,128)S(1)}, bf16[256,768]{1,0:T(8,128)(2,1)S(1)}, bf16[2,256,192]{2,1,0:T(8,128)(2,1)S(1...) custom-call(s32[2]{0:T(128)S(1)} %copy-done.116, ...), custom_call_target="tpu_custom_call" | custom-call | flops 90000000 | bytes 296448 | tf_op jit(solution)/shard_map/dec_attend_back/pallas_call | solution.py:833
  300.7 8.6 %collective-permute-done.28.refs_4_ = bf16[256,768]{1,0:T(8,128)(2,1)S(1)} collective-permute-done((bf16[256,768]{1,0:T(8,128)(2,1)}, bf16[256,768]{1,0:T(8,128)(2,1)S(1)}, u32[]{:S(2)}, u32[]{:S(2)}) %collective-permute-start.28) | collective-permute-done | bytes 393248 | tf_op jit(solution)/shard_map/ppermute | solution.py:705
  313.1 9.4 %enc_attend_back.1 = (f32[256,768]{1,0:T(8,128)S(1)}, f32[1,768]{1,0:T(1,128)S(1)}, bf16[256,768]{1,0:T(8,128)(2,1)S(1)}, bf16[2,256,192]{2,1,0:T(8,128)(2,1)S(1...) custom-call(s32[2]{0:T(128)S(1)} %pad_add_fusion.refs_0_, ...), custom_call_target="tpu_custom_call" | custom-call | flops 90000000 | bytes 278016 | tf_op jit(solution)/shard_map/enc_attend_back/pallas_call | solution.py:833
  341.9 6.9 %collective-permute-done.32.refs_3_ = bf16[256,768]{1,0:T(8,128)(2,1)} collective-permute-done((bf16[256,768]{1,0:T(8,128)(2,1)}, bf16[256,768]{1,0:T(8,128)(2,1)}, u32[]{:S(2)}, u32[]{:S(2)}) %collective-permute-start.32) | collective-permute-done | bytes 393248 | tf_op jit(solution)/shard_map/ppermute | solution.py:705
  350.4 5.7 %collective-permute-done.31.refs_3_ = bf16[256,768]{1,0:T(8,128)(2,1)S(1)} collective-permute-done((bf16[256,768]{1,0:T(8,128)(2,1)}, bf16[256,768]{1,0:T(8,128)(2,1)S(1)}, u32[]{:S(2)}, u32[]{:S(2)}) %collective-permute-start.31) | collective-permute-done | bytes 393248 | tf_op jit(solution)/shard_map/ppermute | solution.py:705
  356.5 3.1 collective-permute-done.35
  371.1 2.8 collective-permute-done.53
  383.5 9.3 %collective-permute-done.37 = bf16[64,768]{1,0:T(8,128)(2,1)S(1)} collective-permute-done((bf16[64,768]{1,0:T(8,128)(2,1)S(1)}, bf16[64,768]{1,0:T(8,128)(2,1)S(1)}, u32[]{:S(2)}, u32[]{:S(2)}) %collective-permute-start.37) | collective-permute-done | bytes 98336 | tf_op jit(solution)/shard_map/ppermute | solution.py:705
  395.4 2.7 collective-permute-done.36
  413.1 3.0 collective-permute-start.58
  433.6 2.8 shards.1
  (636 shorter events, 201.2 us)
Async XLA Ops:
  7.2 110.6 %all-gather.3.cloned.1.call-start = ((), (), s32[]{:S(2)}) async-start(), calls=%async_computation.2 | async-start | bytes 5308416 | tf_op jit(solution)/shard_map/all_gather | solution.py:1504
  11.3 9.5 %collective-permute-start.2 = (bf16[2,24,2816]{2,1,0:T(8,128)(2,1)S(1)}, bf16[2,24,2816]{2,1,0:T(8,128)(2,1)S(1)}, u32[]{:S(2)}, u32[]{:S(2)}) collective-permute-start(bf16[2,24,2816]{2,1,0:T(8,128)(2,1)S(1)} %dynamic-slice_bitcast_fusion), channel_id=1, source_target_pairs={{0,2},{2,0},{1,3},{3,1},{4,6},{6,4},{5,7},{7,5},{8,10},{10,8},{9,1... | collective-permute-start | bytes 811016 | tf_op jit(solution)/shard_map/ppermute | solution.py:705
  23.6 147.5 %all-gather.5.cloned.1.call-start = ((), (), s32[]{:S(2)}) async-start(), calls=%async_computation.3 | async-start | bytes 2654208 | tf_op jit(solution)/shard_map/all_gather | solution.py:1504
  24.1 28.5 %collective-permute-start = (bf16[4,64,768]{2,1,0:T(8,128)(2,1)S(1)}, bf16[4,64,768]{2,1,0:T(8,128)(2,1)S(1)}, u32[]{:S(2)}, u32[]{:S(2)}) collective-permute-start(bf16[4,64,768]{2,1,0:T(8,128)(2,1)S(1)} %pad_maximum_fusion.8), channel_id=1, source_target_pairs={{0,4},{4,0},{1,5},{5,1},{2,6},{6,2},{3,7},{7,3},{8,12},{12,8},{9,1... | collective-permute-start | bytes 1179656 | tf_op jit(solution)/shard_map/ppermute | solution.py:705
  26.3 9.6 %collective-permute-start.5 = (bf16[96,896]{1,0:T(8,128)(2,1)S(1)}, bf16[96,896]{1,0:T(8,128)(2,1)S(1)}, u32[]{:S(2)}, u32[]{:S(2)}) collective-permute-start(bf16[96,896]{1,0:T(8,128)(2,1)S(1)} %fusion.25), channel_id=1, source_target_pairs={{0,8},{8,16},{16,24},{24,0},{1,9},{9,17},{17,25},{25,1},{2,10},{10... | collective-permute-start | bytes 516104 | tf_op jit(solution)/shard_map/ppermute | solution.py:709
  30.6 20.3 %collective-permute-start.6 = (bf16[96,896]{1,0:T(8,128)(2,1)S(1)}, bf16[96,896]{1,0:T(8,128)(2,1)S(1)}, u32[]{:S(2)}, u32[]{:S(2)}) collective-permute-start(bf16[96,896]{1,0:T(8,128)(2,1)S(1)} %fusion.25), channel_id=1, source_target_pairs={{0,16},{8,24},{16,0},{24,8},{1,17},{9,25},{17,1},{25,9},{2,18},{10... | collective-permute-start | bytes 516104 | tf_op jit(solution)/shard_map/ppermute | solution.py:709
  33.5 17.4 %collective-permute-start.7 = (bf16[96,896]{1,0:T(8,128)(2,1)S(1)}, bf16[96,896]{1,0:T(8,128)(2,1)S(1)}, u32[]{:S(2)}, u32[]{:S(2)}) collective-permute-start(bf16[96,896]{1,0:T(8,128)(2,1)S(1)} %fusion.25), channel_id=1, source_target_pairs={{0,24},{8,0},{16,8},{24,16},{1,25},{9,1},{17,9},{25,17},{2,26},{10... | collective-permute-start | bytes 516104 | tf_op jit(solution)/shard_map/ppermute | solution.py:709
  51.0 17.2 %collective-permute-start.8 = (bf16[4,96,896]{2,1,0:T(8,128)(2,1)S(1)}, bf16[4,96,896]{2,1,0:T(8,128)(2,1)S(1)}, u32[]{:S(2)}, u32[]{:S(2)}) collective-permute-start(bf16[4,96,896]{2,1,0:T(8,128)(2,1)S(1)} %bitcast_dynamic-update-slice_fusion), channel_id=1, source_target_pairs={{0,4},{4,0},{1,5},{5,1},{2,6},{6,2},{3,7},{7,3},{8,12},{12,8},{9,1... | collective-permute-start | bytes 2064392 | tf_op jit(solution)/shard_map/ppermute | solution.py:705
  52.8 19.0 %collective-permute-start.1 = (bf16[2,4,64,768]{3,2,1,0:T(8,128)(2,1)S(1)}, bf16[2,4,64,768]{3,2,1,0:T(8,128)(2,1)S(1)}, u32[]{:S(2)}, u32[]{:S(2)}) collective-permute-start(bf16[2,4,64,768]{3,2,1,0:T(8,128)(2,1)S(1)} %pad_maximum_fusion.1), channel_id=1, source_target_pairs={{0,2},{2,0},{1,3},{3,1},{4,6},{6,4},{5,7},{7,5},{8,10},{10,8},{9,1... | collective-permute-start | bytes 2359304 | tf_op jit(solution)/shard_map/ppermute | solution.py:705
  75.8 11.1 %collective-permute-start.20 = (bf16[2,24,1024]{2,1,0:T(8,128)(2,1)S(1)}, bf16[2,24,1024]{2,1,0:T(8,128)(2,1)S(1)}, u32[]{:S(2)}, u32[]{:S(2)}) collective-permute-start(bf16[2,24,1024]{2,1,0:T(8,128)(2,1)S(1)} %fusion.35), channel_id=1, source_target_pairs={{0,1},{1,0},{2,3},{3,2},{4,5},{5,4},{6,7},{7,6},{8,9},{9,8},{10,11... | collective-permute-start | bytes 294920 | tf_op jit(solution)/shard_map/ppermute | solution.py:705
  85.4 11.5 %collective-permute-start.11 = (bf16[256,768]{1,0:T(8,128)(2,1)S(1)}, bf16[256,768]{1,0:T(8,128)(2,1)S(1)}, u32[]{:S(2)}, u32[]{:S(2)}) collective-permute-start(bf16[256,768]{1,0:T(8,128)(2,1)S(1)} %get-tuple-element.147), channel_id=1, source_target_pairs={{0,2},{2,0},{1,3},{3,1},{4,6},{6,4},{5,7},{7,5},{8,10},{10,8},{9,1... | collective-permute-start | bytes 1179656 | tf_op jit(solution)/shard_map/ppermute | solution.py:705
  87.8 206.7 %reduce-scatter.3.cloned.1.call-start = ((), (), s32[]{:S(2)}) async-start(), calls=%async_computation.4 | async-start | bytes 2654208 | tf_op jit(solution)/shard_map/reduce_scatter | solution.py:1596
  120.6 18.8 %collective-permute-start.14 = (bf16[768,1536]{1,0:T(8,128)(2,1)S(1)}, bf16[768,1536]{1,0:T(8,128)(2,1)S(1)}, u32[]{:S(2)}, u32[]{:S(2)}) collective-permute-start(bf16[768,1536]{1,0:T(8,128)(2,1)S(1)} %get-tuple-element.310.refs_4_.refs_6_), channel_id=1, source_target_pairs={{0,1},{1,0},{2,3},{3,2},{4,5},{5,4},{6,7},{7,6},{8,9},{9,8},{10,11... | collective-permute-start | bytes 7077896 | tf_op jit(solution)/shard_map/ppermute | solution.py:705
  136.3 13.0 %collective-permute-start.16 = (bf16[256,768]{1,0:T(8,128)(2,1)S(1)}, bf16[256,768]{1,0:T(8,128)(2,1)S(1)}, u32[]{:S(2)}, u32[]{:S(2)}) collective-permute-start(bf16[256,768]{1,0:T(8,128)(2,1)S(1)} %get-tuple-element.151), channel_id=1, source_target_pairs={{0,2},{2,0},{1,3},{3,1},{4,6},{6,4},{5,7},{7,5},{8,10},{10,8},{9,1... | collective-permute-start | bytes 1179656 | tf_op jit(solution)/shard_map/ppermute | solution.py:705
  142.7 14.6 %collective-permute-start.15 = (bf16[256,768]{1,0:T(8,128)(2,1)S(1)}, bf16[256,768]{1,0:T(8,128)(2,1)S(1)}, u32[]{:S(2)}, u32[]{:S(2)}) collective-permute-start(bf16[256,768]{1,0:T(8,128)(2,1)S(1)} %get-tuple-element.155), channel_id=1, source_target_pairs={{0,2},{2,0},{1,3},{3,1},{4,6},{6,4},{5,7},{7,5},{8,10},{10,8},{9,1... | collective-permute-start | bytes 1179656 | tf_op jit(solution)/shard_map/ppermute | solution.py:705
  171.0 11.7 %collective-permute-start.21 = (bf16[768,1536]{1,0:T(8,128)(2,1)}, bf16[768,1536]{1,0:T(8,128)(2,1)S(1)}, u32[]{:S(2)}, u32[]{:S(2)}) collective-permute-start(bf16[768,1536]{1,0:T(8,128)(2,1)} %all-gather.5.cloned.1.call-done.refs_4_.refs_6_), channel_id=1, source_target_pairs={{0,1},{1,0},{2,3},{3,2},{4,5},{5,4},{6,7},{7,6},{8,9},{9,8},{10,11... | collective-permute-start | bytes 7077896 | tf_op jit(solution)/shard_map/ppermute | solution.py:705
  171.0 11.7 %collective-permute-start.18 = (bf16[256,768]{1,0:T(8,128)(2,1)}, bf16[256,768]{1,0:T(8,128)(2,1)S(1)}, u32[]{:S(2)}, u32[]{:S(2)}) collective-permute-start(bf16[256,768]{1,0:T(8,128)(2,1)} %copy-done.118), channel_id=1, source_target_pairs={{0,2},{2,0},{1,3},{3,1},{4,6},{6,4},{5,7},{7,5},{8,10},{10,8},{9,1... | collective-permute-start | bytes 1179656 | tf_op jit(solution)/shard_map/ppermute | solution.py:705
  199.4 10.8 %collective-permute-start.22 = (bf16[256,768]{1,0:T(8,128)(2,1)S(1)}, bf16[256,768]{1,0:T(8,128)(2,1)S(1)}, u32[]{:S(2)}, u32[]{:S(2)}) collective-permute-start(bf16[256,768]{1,0:T(8,128)(2,1)S(1)} %get-tuple-element.169), channel_id=1, source_target_pairs={{0,2},{2,0},{1,3},{3,1},{4,6},{6,4},{5,7},{7,5},{8,10},{10,8},{9,1... | collective-permute-start | bytes 1179656 | tf_op jit(solution)/shard_map/ppermute | solution.py:705
  214.5 11.5 %collective-permute-start.23 = (bf16[256,768]{1,0:T(8,128)(2,1)S(1)}, bf16[256,768]{1,0:T(8,128)(2,1)S(1)}, u32[]{:S(2)}, u32[]{:S(2)}) collective-permute-start(bf16[256,768]{1,0:T(8,128)(2,1)S(1)} %get-tuple-element.175), channel_id=1, source_target_pairs={{0,2},{2,0},{1,3},{3,1},{4,6},{6,4},{5,7},{7,5},{8,10},{10,8},{9,1... | collective-permute-start | bytes 1179656 | tf_op jit(solution)/shard_map/ppermute | solution.py:705
  226.8 182.1 %reduce-scatter.5.cloned.1.call-start = ((), (), s32[]{:S(2)}) async-start(), calls=%async_computation.5 | async-start | bytes 5308416 | tf_op jit(solution)/shard_map/reduce_scatter | solution.py:1596
  245.8 12.0 %collective-permute-start.26 = (bf16[256,768]{1,0:T(8,128)(2,1)S(1)}, bf16[256,768]{1,0:T(8,128)(2,1)S(1)}, u32[]{:S(2)}, u32[]{:S(2)}) collective-permute-start(bf16[256,768]{1,0:T(8,128)(2,1)S(1)} %get-tuple-element.189), channel_id=1, source_target_pairs={{0,2},{2,0},{1,3},{3,1},{4,6},{6,4},{5,7},{7,5},{8,10},{10,8},{9,1... | collective-permute-start | bytes 1179656 | tf_op jit(solution)/shard_map/ppermute | solution.py:705
  247.2 18.2 %collective-permute-start.27 = (bf16[256,768]{1,0:T(8,128)(2,1)S(1)}, bf16[256,768]{1,0:T(8,128)(2,1)S(1)}, u32[]{:S(2)}, u32[]{:S(2)}) collective-permute-start(bf16[256,768]{1,0:T(8,128)(2,1)S(1)} %get-tuple-element.190), channel_id=1, source_target_pairs={{0,2},{2,0},{1,3},{3,1},{4,6},{6,4},{5,7},{7,5},{8,10},{10,8},{9,1... | collective-permute-start | bytes 1179656 | tf_op jit(solution)/shard_map/ppermute | solution.py:705
  272.0 18.6 %collective-permute-start.41 = (bf16[768,1536]{1,0:T(8,128)(2,1)S(1)}, bf16[768,1536]{1,0:T(8,128)(2,1)S(1)}, u32[]{:S(2)}, u32[]{:S(2)}) collective-permute-start(bf16[768,1536]{1,0:T(8,128)(2,1)S(1)} %get-tuple-element.203), channel_id=1, source_target_pairs={{0,1},{1,0},{2,3},{3,2},{4,5},{5,4},{6,7},{7,6},{8,9},{9,8},{10,11... | collective-permute-start | bytes 7077896 | tf_op jit(solution)/shard_map/ppermute | solution.py:705
  299.2 10.1 %collective-permute-start.28 = (bf16[256,768]{1,0:T(8,128)(2,1)}, bf16[256,768]{1,0:T(8,128)(2,1)S(1)}, u32[]{:S(2)}, u32[]{:S(2)}) collective-permute-start(bf16[256,768]{1,0:T(8,128)(2,1)} %copy-done.117), channel_id=1, source_target_pairs={{0,2},{2,0},{1,3},{3,1},{4,6},{6,4},{5,7},{7,5},{8,10},{10,8},{9,1... | collective-permute-start | bytes 1179656 | tf_op jit(solution)/shard_map/ppermute | solution.py:705
  335.5 24.1 %collective-permute-start.35 = (bf16[4,96,896]{2,1,0:T(8,128)(2,1)}, bf16[4,96,896]{2,1,0:T(8,128)(2,1)}, u32[]{:S(2)}, u32[]{:S(2)}) collective-permute-start(bf16[4,96,896]{2,1,0:T(8,128)(2,1)} %fusion.1), channel_id=1, source_target_pairs={{0,4},{4,0},{1,5},{5,1},{2,6},{6,2},{3,7},{7,3},{8,12},{12,8},{9,1... | collective-permute-start | bytes 2064392 | tf_op jit(solution)/shard_map/ppermute | solution.py:705
  336.5 12.3 %collective-permute-start.32 = (bf16[256,768]{1,0:T(8,128)(2,1)}, bf16[256,768]{1,0:T(8,128)(2,1)}, u32[]{:S(2)}, u32[]{:S(2)}) collective-permute-start(bf16[256,768]{1,0:T(8,128)(2,1)} %get-tuple-element.230), channel_id=1, source_target_pairs={{0,2},{2,0},{1,3},{3,1},{4,6},{6,4},{5,7},{7,5},{8,10},{10,8},{9,1... | collective-permute-start | bytes 1179656 | tf_op jit(solution)/shard_map/ppermute | solution.py:705
  338.0 18.0 %collective-permute-start.31 = (bf16[256,768]{1,0:T(8,128)(2,1)}, bf16[256,768]{1,0:T(8,128)(2,1)S(1)}, u32[]{:S(2)}, u32[]{:S(2)}) collective-permute-start(bf16[256,768]{1,0:T(8,128)(2,1)} %get-tuple-element.220), channel_id=1, source_target_pairs={{0,2},{2,0},{1,3},{3,1},{4,6},{6,4},{5,7},{7,5},{8,10},{10,8},{9,1... | collective-permute-start | bytes 1179656 | tf_op jit(solution)/shard_map/ppermute | solution.py:705
  362.1 38.5 %collective-permute-start.43 = (bf16[96,896]{1,0:T(8,128)(2,1)S(1)}, bf16[96,896]{1,0:T(8,128)(2,1)S(1)}, u32[]{:S(2)}, u32[]{:S(2)}) collective-permute-start(bf16[96,896]{1,0:T(8,128)(2,1)S(1)} %get-tuple-element.330), channel_id=1, source_target_pairs={{0,8},{8,16},{16,24},{24,0},{1,9},{9,17},{17,25},{25,1},{2,10},{10... | collective-permute-start | bytes 516104 | tf_op jit(solution)/shard_map/ppermute | solution.py:709
  363.4 37.1 %collective-permute-start.44 = (bf16[96,896]{1,0:T(8,128)(2,1)S(1)}, bf16[96,896]{1,0:T(8,128)(2,1)S(1)}, u32[]{:S(2)}, u32[]{:S(2)}) collective-permute-start(bf16[96,896]{1,0:T(8,128)(2,1)S(1)} %get-tuple-element.332), channel_id=1, source_target_pairs={{0,16},{8,24},{16,0},{24,8},{1,17},{9,25},{17,1},{25,9},{2,18},{10... | collective-permute-start | bytes 516104 | tf_op jit(solution)/shard_map/ppermute | solution.py:709
  379.6 20.9 %collective-permute-start.45 = (bf16[96,896]{1,0:T(8,128)(2,1)S(1)}, bf16[96,896]{1,0:T(8,128)(2,1)S(1)}, u32[]{:S(2)}, u32[]{:S(2)}) collective-permute-start(bf16[96,896]{1,0:T(8,128)(2,1)S(1)} %get-tuple-element.331), channel_id=1, source_target_pairs={{0,24},{8,0},{16,8},{24,16},{1,25},{9,1},{17,9},{25,17},{2,26},{10... | collective-permute-start | bytes 516104 | tf_op jit(solution)/shard_map/ppermute | solution.py:709
  381.5 22.2 %collective-permute-start.39 = (f32[64,768]{1,0:T(8,128)}, f32[64,768]{1,0:T(8,128)}, u32[]{:S(2)}, u32[]{:S(2)}) collective-permute-start(f32[64,768]{1,0:T(8,128)} %dynamic-slice_bitcast_fusion.2), channel_id=1, source_target_pairs={{0,4},{4,0},{1,5},{5,1},{2,6},{6,2},{3,7},{7,3},{8,12},{12,8},{9,1... | collective-permute-start | bytes 589832 | tf_op jit(solution)/shard_map/ppermute | solution.py:705
  382.1 10.7 %collective-permute-start.37 = (bf16[64,768]{1,0:T(8,128)(2,1)S(1)}, bf16[64,768]{1,0:T(8,128)(2,1)S(1)}, u32[]{:S(2)}, u32[]{:S(2)}) collective-permute-start(bf16[64,768]{1,0:T(8,128)(2,1)S(1)} %dynamic-slice_bitcast_fusion.8), channel_id=1, source_target_pairs={{0,4},{4,0},{1,5},{5,1},{2,6},{6,2},{3,7},{7,3},{8,12},{12,8},{9,1... | collective-permute-start | bytes 294920 | tf_op jit(solution)/shard_map/ppermute | solution.py:705
  (185 other events, 1240.0 us)
Sparse Core Ops, SparseCore 0:
  23.7 94.1 all-gather.2
  120.0 50.9 all-gather.4
  226.9 67.4 reduce-scatter.2
  299.3 104.4 reduce-scatter.4
